TPU v7x, 32 devices: a whole 2x2x4 slice. The times are simulated.
32 devices in a mesh: dp: 4 (over y, x), row: 4 (over z), col: 2 (over core).
Axes of the slice: x: 2, y: 2, z: 4, core: 2. Of those that a mesh axis runs over, the one named last changes fastest.
Arguments:
- hidden: bfloat16 [16384, 1024], P(('dp', 'row'), 'col'), may hold values from -6 to 6
- segments: int32 [16, 1024], P(('dp', 'row')), may hold values from 0 to 3, never falling along the last dimension, each value on 1 to 512 neighbouring positions
- ln1_gain: bfloat16 [1024], P('col'), may hold values from 0.5 to 1.5
- ln1_bias: bfloat16 [1024], P('col'), may hold values from -3 to 3
- qkv_weight: bfloat16 [1024, 3072], P('row', 'col'), may hold values from -0.25 to 0.25
- qkv_bias: bfloat16 [3072], P('col'), may hold values from -2 to 2
- out_weight: bfloat16 [1024, 1024], P('col', 'row'), may hold values from -0.75 to 0.75
- out_bias: bfloat16 [1024], P('col'), may hold values from -2 to 2
- ln2_gain: bfloat16 [1024], P('col'), may hold values from 0.5 to 1.5
- ln2_bias: bfloat16 [1024], P('col'), may hold values from -3 to 3
- up_weight: bfloat16 [1024, 4096], P('row', 'col'), may hold values from -0.1875 to 0.1875
- up_bias: bfloat16 [4096], P('col'), may hold values from -2 to 2
- down_weight: bfloat16 [4096, 1024], P('col', 'row'), may hold values from -0.125 to 0.125
- down_bias: bfloat16 [1024], P('col'), may hold values from -2 to 2
- cotangent: bfloat16 [16384, 1024], P(('dp', 'row'), 'col'), may hold values from -6 to 6
Outputs:
- output: float32 [16384, 1024], P(('dp', 'row'), 'col')
- input_grad: float32 [16384, 1024], P(('dp', 'row'), 'col')
- ln1_gain_grad: float32 [1024], P('col')
- ln1_bias_grad: float32 [1024], P('col')
- qkv_weight_grad: float32 [1024, 3072], P('row', 'col')
- qkv_bias_grad: float32 [3072], P('col')
- out_weight_grad: float32 [1024, 1024], P('col', 'row')
- out_bias_grad: float32 [1024], P('col')
- ln2_gain_grad: float32 [1024], P('col')
- ln2_bias_grad: float32 [1024], P('col')
- up_weight_grad: float32 [1024, 4096], P('row', 'col')
- up_bias_grad: float32 [4096], P('col')
- down_weight_grad: float32 [4096, 1024], P('col', 'row')
- down_bias_grad: float32 [1024], P('col')
Inputs may be any that keep to these rules, and one draw needn't show every extreme that they name: `segments`: segment numbers never fall along a sequence; a document holds at most 512 tokens.
All inputs are finite; a program needn't handle non-finite values.
Results may differ from a plain program's by a relative error of at most 0.012.
The roundings to bfloat16 on the way count: a program that leaves them out, or rounds other values in their place, can miss the bound.
Values may be sent and summed in bfloat16 or wider, within the bound.
A program may use at most 256 MiB of HBM per device.

v0:
```python
from functools import partial

import jax
import jax.numpy as jnp
from jax import lax
from jax.sharding import PartitionSpec as P

HEAD_DIM = 64
ROT = 16


EPS = 1e-05


def normalize(values, gain_vec, shift_vec):
    centred = values - jnp.mean(values, axis=-1, keepdims=True)
    variance = jnp.mean(centred * centred, axis=-1, keepdims=True)
    inv_std = lax.rsqrt(variance + EPS)
    unit_rows = centred * inv_std
    return (unit_rows * gain_vec + shift_vec, unit_rows, inv_std)


def doc_positions(segments):
    length = segments.shape[-1]
    places = jnp.arange(length, dtype=jnp.int32)
    changed = jnp.concatenate(
        [jnp.ones(segments.shape[:-1] + (1,), dtype=bool), segments[..., 1:] != segments[..., :-1]],
        axis=-1,
    )
    starts = lax.cummax(jnp.where(changed, places, jnp.zeros_like(places)), axis=segments.ndim - 1)
    return places - starts


def rotary_tables(positions):
    frequency = 10000.0 ** (-jnp.arange(0, ROT, 2, dtype=jnp.float32) / ROT)
    angles = positions.astype(jnp.float32)[..., None] * frequency
    angles = jnp.concatenate([angles, angles], axis=-1)
    return (jnp.cos(angles), jnp.sin(angles))


def rotate(values, cos_table, sine_table):
    rot_part = values[..., :ROT]
    turned = jnp.concatenate([-rot_part[..., ROT // 2 :], rot_part[..., : ROT // 2]], axis=-1)
    return jnp.concatenate([rot_part * cos_table + turned * sine_table, values[..., ROT:]], axis=-1)


def unrotate(grad_in, cos_table, sine_table):
    rot_part = grad_in[..., :ROT]
    with_sine = rot_part * sine_table
    back_turn = jnp.concatenate([with_sine[..., ROT // 2 :], -with_sine[..., : ROT // 2]], axis=-1)
    return jnp.concatenate([rot_part * cos_table + back_turn, grad_in[..., ROT:]], axis=-1)


def block_scores(query_rows, key_vecs, segment_row, offset):
    length = key_vecs.shape[0]
    block_rows = query_rows.shape[0]
    scores = jnp.einsum(
        "qhd,khd->hqk", query_rows, key_vecs, preferred_element_type=jnp.float32
    ) * HEAD_DIM ** (-0.5)
    query_places = offset + jnp.arange(block_rows)
    key_places = jnp.arange(length)
    query_segs = segment_row[offset : offset + block_rows]
    allowed = (query_segs[:, None] == segment_row[None, :]) & (
        query_places[:, None] >= key_places[None, :]
    )
    return jnp.where(allowed[None], scores, -1e30)


def attend_forward(pieces):
    queries, key_vecs, value_vecs, segment_row = pieces
    length = queries.shape[0]
    block_rows = min(512, length)
    outputs = []
    log_parts = []
    for offset in range(0, length, block_rows):
        scores = block_scores(queries[offset : offset + block_rows], key_vecs, segment_row, offset)
        row_max = jnp.max(scores, axis=-1, keepdims=True)
        powers = jnp.exp(scores - row_max)
        totals = jnp.sum(powers, axis=-1, keepdims=True)
        attn_probs = (powers / totals).astype(jnp.bfloat16)
        outputs.append(
            jnp.einsum("hqk,khd->qhd", attn_probs, value_vecs, preferred_element_type=jnp.float32)
        )
        log_parts.append((row_max + jnp.log(totals))[..., 0])
    return (jnp.concatenate(outputs, axis=0), jnp.concatenate(log_parts, axis=1))


def attend_backward(pieces):
    queries, key_vecs, value_vecs, segment_row, grad_context, log_sums = pieces
    length = queries.shape[0]
    block_rows = min(512, length)
    factor = HEAD_DIM ** (-0.5)
    grad_queries = []
    grad_keys = jnp.zeros(key_vecs.shape, jnp.float32)
    grad_values = jnp.zeros(value_vecs.shape, jnp.float32)
    for offset in range(0, length, block_rows):
        query_rows = queries[offset : offset + block_rows]
        cot_rows = grad_context[offset : offset + block_rows]
        scores = block_scores(query_rows, key_vecs, segment_row, offset)
        attn_probs = jnp.exp(scores - log_sums[:, offset : offset + block_rows, None])
        grad_probs = jnp.einsum(
            "qhd,khd->hqk", cot_rows, value_vecs, preferred_element_type=jnp.float32
        )
        row_dots = jnp.sum(grad_probs * attn_probs, axis=-1, keepdims=True)
        grad_scores = (attn_probs * (grad_probs - row_dots)).astype(jnp.bfloat16)
        grad_queries.append(
            jnp.einsum("hqk,khd->qhd", grad_scores, key_vecs, preferred_element_type=jnp.float32)
            * factor
        )
        grad_keys = (
            grad_keys
            + jnp.einsum(
                "hqk,qhd->khd", grad_scores, query_rows, preferred_element_type=jnp.float32
            )
            * factor
        )
        grad_values = grad_values + jnp.einsum(
            "hqk,qhd->khd",
            attn_probs.astype(jnp.bfloat16),
            cot_rows,
            preferred_element_type=jnp.float32,
        )
    return (jnp.concatenate(grad_queries, axis=0), grad_keys, grad_values)


def regroup(matrix, split_axis, row_count, group_count):
    dims_in = matrix.shape
    split_dims = (
        dims_in[:split_axis]
        + (row_count, group_count, dims_in[split_axis] // (row_count * group_count))
        + dims_in[split_axis + 1 :]
    )
    return jnp.swapaxes(matrix.reshape(split_dims), split_axis, split_axis + 1).reshape(dims_in)


def local(
    hidden,
    segments,
    ln1_gain,
    ln1_bias,
    qkv_weight,
    qkv_bias,
    out_weight,
    out_bias,
    ln2_gain,
    ln2_bias,
    up_weight,
    up_bias,
    down_weight,
    down_bias,
    cotangent,
):
    seq_count, length = segments.shape
    tok_rows = seq_count * length
    half_width = hidden.shape[1]
    start_col = lax.axis_index("col") * half_width
    inputs_all, cot_all, gain_one, shift_one, gain_two, shift_two = (
        lax.all_gather(hidden, "col", axis=1, tiled=True),
        lax.all_gather(cotangent, "col", axis=1, tiled=True),
        lax.all_gather(ln1_gain, "col", axis=0, tiled=True),
        lax.all_gather(ln1_bias, "col", axis=0, tiled=True),
        lax.all_gather(ln2_gain, "col", axis=0, tiled=True),
        lax.all_gather(ln2_bias, "col", axis=0, tiled=True),
    )
    qkv_all, out_all, up_all, down_all = (
        lax.all_gather(qkv_weight, "row", axis=0, tiled=True),
        lax.all_gather(out_weight, "row", axis=1, tiled=True),
        lax.all_gather(up_weight, "row", axis=0, tiled=True),
        lax.all_gather(down_weight, "row", axis=1, tiled=True),
    )
    heads_here = qkv_all.shape[1] // (3 * HEAD_DIM)
    inputs_wide = inputs_all.astype(jnp.float32)
    normed_one, unit_one, inv_one = normalize(
        inputs_wide, gain_one.astype(jnp.float32), shift_one.astype(jnp.float32)
    )
    act_one = normed_one.astype(jnp.bfloat16)
    qkv_rows = jnp.dot(act_one, qkv_all, preferred_element_type=jnp.float32) + qkv_bias.astype(
        jnp.float32
    )
    qkv_rows = qkv_rows.reshape(tok_rows, heads_here, 3, HEAD_DIM)
    cos_table, sine_table = rotary_tables(doc_positions(segments).reshape(tok_rows))
    cos_table = cos_table[:, None, :]
    sine_table = sine_table[:, None, :]
    queries = rotate(qkv_rows[:, :, 0], cos_table, sine_table).astype(jnp.bfloat16)
    key_vecs = rotate(qkv_rows[:, :, 1], cos_table, sine_table).astype(jnp.bfloat16)
    value_vecs = qkv_rows[:, :, 2].astype(jnp.bfloat16)
    seq_shape = (seq_count, length, heads_here, HEAD_DIM)
    queries = queries.reshape(seq_shape)
    key_vecs = key_vecs.reshape(seq_shape)
    value_vecs = value_vecs.reshape(seq_shape)
    context, log_sums = lax.map(attend_forward, (queries, key_vecs, value_vecs, segments))
    context = context.reshape(tok_rows, heads_here * HEAD_DIM).astype(jnp.bfloat16)
    normed_two, unit_two, inv_two = normalize(
        inputs_wide, gain_two.astype(jnp.float32), shift_two.astype(jnp.float32)
    )
    act_two = normed_two.astype(jnp.bfloat16)
    up_proj = jnp.dot(act_two, up_all, preferred_element_type=jnp.float32) + up_bias.astype(
        jnp.float32
    )
    gelu_exact = partial(jax.nn.gelu, approximate=False)
    hidden_act = gelu_exact(up_proj).astype(jnp.bfloat16)
    branch_sum = jnp.dot(context, out_all, preferred_element_type=jnp.float32) + jnp.dot(
        hidden_act, down_all, preferred_element_type=jnp.float32
    )
    summed = lax.psum_scatter(
        branch_sum.astype(jnp.bfloat16), "col", scatter_dimension=1, tiled=True
    ).astype(jnp.float32)
    cot_local = cotangent.astype(jnp.float32)
    output = (
        hidden.astype(jnp.float32)
        + summed
        + (out_bias.astype(jnp.float32) + down_bias.astype(jnp.float32))
    )
    bias_grad = jnp.sum(cot_local, axis=0)
    grad_out_weight = jnp.dot(context.T, cot_all, preferred_element_type=jnp.float32)
    grad_down_weight = jnp.dot(hidden_act.T, cot_all, preferred_element_type=jnp.float32)
    grad_context = jnp.dot(cot_all, out_all.T, preferred_element_type=jnp.float32).astype(
        jnp.bfloat16
    )
    grad_hidden = jnp.dot(cot_all, down_all.T, preferred_element_type=jnp.float32)
    gelu_pull = jax.vjp(gelu_exact, up_proj)[1]
    grad_up = gelu_pull(grad_hidden)[0].astype(jnp.bfloat16)
    grad_queries, grad_keys, grad_values = lax.map(
        attend_backward,
        (queries, key_vecs, value_vecs, segments, grad_context.reshape(seq_shape), log_sums),
    )
    flat_shape = (tok_rows, heads_here, HEAD_DIM)
    grad_queries = unrotate(grad_queries.reshape(flat_shape), cos_table, sine_table)
    grad_keys = unrotate(grad_keys.reshape(flat_shape), cos_table, sine_table)
    grad_mixed = jnp.stack([grad_queries, grad_keys, grad_values.reshape(flat_shape)], axis=2)
    grad_mixed = grad_mixed.reshape(tok_rows, 3 * heads_here * HEAD_DIM).astype(jnp.bfloat16)
    grad_qkv_weight = jnp.dot(act_one.T, grad_mixed, preferred_element_type=jnp.float32)
    grad_up_weight = jnp.dot(act_two.T, grad_up, preferred_element_type=jnp.float32)
    grad_act_one = jnp.dot(grad_mixed, qkv_all.T, preferred_element_type=jnp.float32)
    grad_act_two = jnp.dot(grad_up, up_all.T, preferred_element_type=jnp.float32)
    unit_one_half = lax.dynamic_slice_in_dim(unit_one, start_col, half_width, 1)
    unit_two_half = lax.dynamic_slice_in_dim(unit_two, start_col, half_width, 1)
    full_one, full_two = (
        lax.psum(grad_act_one.astype(jnp.bfloat16), "col").astype(jnp.float32),
        lax.psum(grad_act_two.astype(jnp.bfloat16), "col").astype(jnp.float32),
    )
    wide_one = full_one * gain_one.astype(jnp.float32)
    wide_two = full_two * gain_two.astype(jnp.float32)
    row_sums = jnp.stack(
        [
            jnp.mean(wide_one, axis=1),
            jnp.mean(wide_one * unit_one, axis=1),
            jnp.mean(wide_two, axis=1),
            jnp.mean(wide_two * unit_two, axis=1),
        ]
    )
    grad_one = lax.dynamic_slice_in_dim(full_one, start_col, half_width, 1)
    grad_two = lax.dynamic_slice_in_dim(full_two, start_col, half_width, 1)
    scaled_one = lax.dynamic_slice_in_dim(wide_one, start_col, half_width, 1)
    scaled_two = lax.dynamic_slice_in_dim(wide_two, start_col, half_width, 1)
    input_grad = cot_local + inv_one * (
        scaled_one - row_sums[0][:, None] - unit_one_half * row_sums[1][:, None]
    )
    input_grad = input_grad + inv_two * (
        scaled_two - row_sums[2][:, None] - unit_two_half * row_sums[3][:, None]
    )
    (
        qkv_bias_grad,
        up_bias_grad,
        outer_bias_grad,
        gain_one_grad,
        shift_one_grad,
        gain_two_grad,
        shift_two_grad,
    ) = lax.psum(
        (
            jnp.sum(grad_mixed.astype(jnp.float32), axis=0),
            jnp.sum(grad_up.astype(jnp.float32), axis=0),
            bias_grad,
            jnp.sum(grad_one * unit_one_half, axis=0),
            jnp.sum(grad_one, axis=0),
            jnp.sum(grad_two * unit_two_half, axis=0),
            jnp.sum(grad_two, axis=0),
        ),
        ("dp", "row"),
    )
    row_count = lax.axis_size("row")
    group_count = lax.axis_size("dp")
    piece_qkv, piece_out, piece_up, piece_down = (
        lax.psum_scatter(
            regroup(grad_qkv_weight, 0, row_count, group_count),
            ("dp", "row"),
            scatter_dimension=0,
            tiled=True,
        ),
        lax.psum_scatter(
            regroup(grad_out_weight, 1, row_count, group_count),
            ("dp", "row"),
            scatter_dimension=1,
            tiled=True,
        ),
        lax.psum_scatter(
            regroup(grad_up_weight, 0, row_count, group_count),
            ("dp", "row"),
            scatter_dimension=0,
            tiled=True,
        ),
        lax.psum_scatter(
            regroup(grad_down_weight, 1, row_count, group_count),
            ("dp", "row"),
            scatter_dimension=1,
            tiled=True,
        ),
    )
    shard_qkv, shard_out, shard_up, shard_down = (
        lax.all_gather(piece_qkv.astype(jnp.bfloat16), "dp", axis=0, tiled=True).astype(
            piece_qkv.dtype
        ),
        lax.all_gather(piece_out.astype(jnp.bfloat16), "dp", axis=1, tiled=True).astype(
            piece_out.dtype
        ),
        lax.all_gather(piece_up.astype(jnp.bfloat16), "dp", axis=0, tiled=True).astype(
            piece_up.dtype
        ),
        lax.all_gather(piece_down.astype(jnp.bfloat16), "dp", axis=1, tiled=True).astype(
            piece_down.dtype
        ),
    )
    return (
        output,
        input_grad,
        gain_one_grad,
        shift_one_grad,
        shard_qkv,
        qkv_bias_grad,
        shard_out,
        outer_bias_grad,
        gain_two_grad,
        shift_two_grad,
        shard_up,
        up_bias_grad,
        shard_down,
        outer_bias_grad,
    )


def solution(mesh):
    placed = (
        P(("dp", "row"), "col"),
        P(("dp", "row"), None),
        P("col"),
        P("col"),
        P("row", "col"),
        P("col"),
        P("col", "row"),
        P("col"),
        P("col"),
        P("col"),
        P("row", "col"),
        P("col"),
        P("col", "row"),
        P("col"),
        P(("dp", "row"), "col"),
    )
    return jax.shard_map(
        local,
        mesh=mesh,
        in_specs=placed,
        out_specs=(
            P(("dp", "row"), "col"),
            P(("dp", "row"), "col"),
            P("col"),
            P("col"),
            P("row", "col"),
            P("col"),
            P("col", "row"),
            P("col"),
            P("col"),
            P("col"),
            P("row", "col"),
            P("col"),
            P("col", "row"),
            P("col"),
        ),
        check_vma=False,
    )
```

profile of v0, /device:TPU:0, one launch (start us, length us, event | category | flops | bytes accessed | tf_op | source)
XLA Modules:
  0.0 1039.6 jit_solution(9564536685548556324)
XLA Ops:
  27.3 28.6 %all-gather.17.cloned.1.call-done = bf16[512,1024]{1,0:T(8,128)(2,1)} async-done(((bf16[512,256]{1,0:T(8,128)(2,1)}), bf16[512,1024]{1,0:T(8,128)(2,1)}) %all-gather.17.cloned.1.call-update) | async-done | bytes 1048592 | tf_op jit(solution)/shard_map/all_gather | solution.py:167
  55.9 10.5 %all-gather.23.cloned.1.call-done = bf16[1024,1024]{1,0:T(8,128)(2,1)} async-done(((bf16[1024,512]{1,0:T(8,128)(2,1)}), bf16[1024,1024]{1,0:T(8,128)(2,1)}) %all-gather.23.cloned.1.call-update) | async-done | bytes 2097168 | tf_op jit(solution)/shard_map/all_gather | solution.py:159
  70.4 62.1 %all-gather.15.cloned.1.call-done = bf16[1024,1536]{1,0:T(8,128)(2,1)} async-done(((bf16[256,1536]{1,0:T(8,128)(2,1)}), bf16[1024,1536]{1,0:T(8,128)(2,1)}) %all-gather.15.cloned.1.call-update) | async-done | bytes 3145744 | tf_op jit(solution)/shard_map/all_gather | solution.py:166
  132.5 7.5 convolution_add_fusion
  140.0 6.7 copy.54
  168.9 11.9 %multiply_reduce_fusion.1 = (f32[8,512]{1,0:T(8,128)S(1)}, f32[8,512,1024]{2,1,0:T(8,128)}) fusion(f32[8,512,1024]{2,1,0:T(8,128)} %copy-done.1, f32[8,512]{1,0:T(8,128)S(1)} %log_add_fusion.1, bf16[512,8,64]{0,2,1:T(8,128)(2,1)S(1)} %bitcast.121, f32[1024,8,3,64]{0,3,2,1:T(8,128)} %bitcast.111), kind=kOutput, calls=%fused_computation.4 | convolution fusion | flops 549449728 | bytes 35160064 | tf_op jit(solution)/shard_map/while/body/eval_jaxpr/qhd,khd->hqk/dot_general | solution.py:101
  180.8 11.9 %multiply_convert_fusion.1 = bf16[8,512,1024]{2,1,0:T(8,128)(2,1)S(1)} fusion(f32[8,512,1024]{2,1,0:T(8,128)} %get-tuple-element.151, f32[8,512,1024]{2,1,0:T(8,128)} %copy-done.1, f32[8,512]{1,0:T(8,128)S(1)} %get-tuple-element.150, f32[8,512]{1,0:T(8,128)S(1)} %log_add_fusion.1), kind=kLoop, calls=%fused_computation.3 | loop fusion | flops 16777216 | bytes 41975808 | tf_op jit(solution)/shard_map/while/body/eval_jaxpr/convert_element_type | solution.py:105
  194.3 11.8 %multiply_reduce_fusion = (f32[8,512]{1,0:T(8,128)S(1)}, f32[8,512,1024]{2,1,0:T(8,128)}) fusion(f32[8,512,1024]{2,1,0:T(8,128)} %copy-done, f32[8,512]{1,0:T(8,128)S(1)} %log_add_fusion, bf16[512,8,64]{0,2,1:T(8,128)(2,1)S(1)} %bitcast.123, f32[1024,8,3,64]{0,3,2,1:T(8,128)} %bitcast.112), kind=kOutput, calls=%fused_computation.1 | convolution fusion | flops 549449728 | bytes 35160064 | tf_op jit(solution)/shard_map/while/body/eval_jaxpr/qhd,khd->hqk/dot_general | solution.py:101
  206.1 12.2 %multiply_convert_fusion = bf16[8,512,1024]{2,1,0:T(8,128)(2,1)S(1)} fusion(f32[8,512,1024]{2,1,0:T(8,128)} %get-tuple-element.153, f32[8,512,1024]{2,1,0:T(8,128)} %copy-done, f32[8,512]{1,0:T(8,128)S(1)} %get-tuple-element.152, f32[8,512]{1,0:T(8,128)S(1)} %log_add_fusion), kind=kLoop, calls=%fused_computation | loop fusion | flops 16777216 | bytes 41975808 | tf_op jit(solution)/shard_map/while/body/eval_jaxpr/convert_element_type | solution.py:105
  224.2 6.4 fusion.28
  240.5 7.5 add_bitcast_fusion
  257.0 9.5 fusion.53
  266.5 27.4 %all-gather.21.cloned.1.call-done = bf16[2048,1024]{1,0:T(8,128)(2,1)} async-done(((bf16[2048,256]{1,0:T(8,128)(2,1)}), bf16[2048,1024]{1,0:T(8,128)(2,1)}) %all-gather.21.cloned.1.call-update) | async-done | bytes 4194320 | tf_op jit(solution)/shard_map/all_gather | solution.py:169
  293.9 27.9 %convert_reduce_fusion = (f32[2048]{0:T(1024)S(1)}, bf16[1024,2048]{1,0:T(8,128)(2,1)S(1)}, f32[1024,2048]{1,0:T(8,128)}) fusion(f32[1024,2048]{1,0:T(8,128)} %fusion.53, f32[2048]{0:T(1024)S(1)} %convert_element_type.170, bf16[1024,1024]{1,0:T(8,128)(2,1)} %all-gather.23.cloned.1.call-done, bf16[2048,1024]{1,0:T(8,128)(2,1)} %all-gather.21.cloned.1.call-done), kind=kOutput, calls=%fused_computation.20 | convolution fusion | flops 4452251648 | bytes 27279360 | tf_op jit(solution)/shard_map/dot_general | solution.py:220
  323.8 5.7 convolution_convert_fusion
  329.8 11.0 %multiply_convert_fusion.2 = bf16[1024,2048]{1,0:T(8,128)(2,1)} fusion(f32[1024,2048]{1,0:T(8,128)} %get-tuple-element.112, f32[1024,2048]{1,0:T(8,128)} %fusion.53, f32[2048]{0:T(1024)S(1)} %convert_element_type.170), kind=kLoop, calls=%fused_computation.24 | loop fusion | flops 8388608 | bytes 20979712 | tf_op jit(solution)/shard_map/convert_element_type | solution.py:201
  340.9 6.6 fusion.68
  355.8 8.1 fusion.30
  365.0 8.5 fusion.31
  379.4 7.0 fusion.52
  390.5 7.7 fusion.67
  401.0 8.5 multiply_reduce_fusion.3
  421.9 120.5 %reduce-scatter.14.cloned.1.call-done = f32[2048,64]{0,1:T(8,128)} async-done(((f32[2048,1024]{0,1:T(8,128)}), f32[2048,64]{0,1:T(8,128)}) %reduce-scatter.14.cloned.1.call-update) | async-done | bytes 524304 | tf_op jit(solution)/shard_map/reduce_scatter | solution.py:303
  544.4 83.0 %reduce-scatter.10.cloned.1.call-done = f32[512,64]{0,1:T(8,128)} async-done(((f32[512,1024]{0,1:T(8,128)}), f32[512,64]{0,1:T(8,128)}) %reduce-scatter.10.cloned.1.call-update) | async-done | bytes 131088 | tf_op jit(solution)/shard_map/reduce_scatter | solution.py:291
  628.2 8.7 all_gather.53
  644.4 164.0 %reduce-scatter.12.cloned.1.call-done = f32[64,2048]{1,0:T(8,128)} async-done(((f32[1024,2048]{1,0:T(8,128)}), f32[64,2048]{1,0:T(8,128)}) %reduce-scatter.12.cloned.1.call-update) | async-done | bytes 524304 | tf_op jit(solution)/shard_map/reduce_scatter | solution.py:297
  810.3 5.8 dynamic-slice_reduce_fusion
  816.1 74.1 %all-reduce = (f32[512]{0:T(512)}, f32[512]{0:T(512)}, f32[1536]{0:T(1024)}, f32[512]{0:T(512)S(1)}, f32[512]{0:T(512)}, /*index=5*/f32[512]{0:T(512)}, f32[2048]{0:T(1024)}) all-reduce(f32[512]{0:T(512)S(1)} %get-tuple-element.95, f32[512]{0:T(512)S(1)} %get-tuple-element.96, ...), channel_id=1, replica_groups=mesh['dp'=4,'row'=4,'col'=2] {'dp','row'}, use_global_device_ids=true, to_apply=%region_18.19 | all-reduce | flops 6144 | bytes 49152 | tf_op jit(solution)/shard_map/psum | solution.py:270
  893.1 78.8 %reduce-scatter.8.cloned.1.call-done = f32[64,1536]{1,0:T(8,128)} async-done(((f32[1024,1536]{1,0:T(8,128)}), f32[64,1536]{1,0:T(8,128)}) %reduce-scatter.8.cloned.1.call-update) | async-done | bytes 393232 | tf_op jit(solution)/shard_map/reduce_scatter | solution.py:285
  972.9 14.4 %all_gather.52 = bf16[256,1536]{1,0:T(8,128)(2,1)S(1)} all-gather(bf16[64,1536]{1,0:T(8,128)(2,1)S(1)} %convert_element_type.189), channel_id=1, replica_groups=mesh['dp'=4,'row'=4,'col'=2] {'dp'}, dimensions={0}, use_global_device_ids=true | all-gather | bytes 983040 | tf_op jit(solution)/shard_map/all_gather | solution.py:311
  988.6 11.6 %all-gather.27.cloned.1.call-done = bf16[2048,256]{0,1:T(8,128)(2,1)} async-done(((bf16[2048,64]{0,1:T(8,128)(2,1)}), bf16[2048,256]{0,1:T(8,128)(2,1)}) %all-gather.27.cloned.1.call-update) | async-done | bytes 1048592 | tf_op jit(solution)/shard_map/all_gather | solution.py:320
  1002.8 26.4 %all-gather.25.cloned.1.call-done = bf16[256,2048]{1,0:T(8,128)(2,1)} async-done(((bf16[64,2048]{1,0:T(8,128)(2,1)}), bf16[256,2048]{1,0:T(8,128)(2,1)}) %all-gather.25.cloned.1.call-update) | async-done | bytes 1048592 | tf_op jit(solution)/shard_map/all_gather | solution.py:317
  (230 shorter events, 132.1 us)
Async XLA Ops:
  7.2 10.3 copy-start.42
  7.2 13.6 %copy-start.35 = (bf16[2048]{0:T(1024)(128)(2,1)S(1)}, bf16[2048]{0:T(1024)(128)(2,1)}, u32[]{:S(2)}) copy-start(bf16[2048]{0:T(1024)(128)(2,1)} %param.26) | copy-start | bytes 12292
  7.2 13.6 %copy-start.36 = (bf16[1536]{0:T(1024)(128)(2,1)S(1)}, bf16[1536]{0:T(1024)(128)(2,1)}, u32[]{:S(2)}) copy-start(bf16[1536]{0:T(1024)(128)(2,1)} %param.20) | copy-start | bytes 9220
  7.3 15.8 %all-gather.13.cloned.1.call-start = ((), (), s32[]{:S(2)}) async-start(), calls=%async_computation.5 | async-start | bytes 3145728 | tf_op jit(solution)/shard_map/all_gather | solution.py:158
  8.0 47.9 %all-gather.17.cloned.1.call-start = ((), (), s32[]{:S(2)}) async-start(), calls=%async_computation.7 | async-start | bytes 1310720 | tf_op jit(solution)/shard_map/all_gather | solution.py:167
  8.7 57.6 %all-gather.23.cloned.1.call-start = ((), (), s32[]{:S(2)}) async-start(), calls=%async_computation.11 | async-start | bytes 3145728 | tf_op jit(solution)/shard_map/all_gather | solution.py:159
  9.5 123.0 %all-gather.15.cloned.1.call-start = ((), (), s32[]{:S(2)}) async-start(), calls=%async_computation.6 | async-start | bytes 3932160 | tf_op jit(solution)/shard_map/all_gather | solution.py:166
  10.0 247.0 %all-gather.19.cloned.1.call-start = ((), (), s32[]{:S(2)}) async-start(), calls=%async_computation.8 | async-start | bytes 5242880 | tf_op jit(solution)/shard_map/all_gather | solution.py:168
  10.6 283.3 %all-gather.21.cloned.1.call-start = ((), (), s32[]{:S(2)}) async-start(), calls=%async_computation.9 | async-start | bytes 5242880 | tf_op jit(solution)/shard_map/all_gather | solution.py:169
  11.2 389.8 %all-reduce.4.cloned.1.call-start = ((), (), s32[]{:S(2)}) async-start(), calls=%async_computation.18 | async-start | bytes 8388608 | tf_op jit(solution)/shard_map/psum | solution.py:240
  13.3 119.2 %copy-start.30 = (f32[2,1,512]{2,1,0:T(1,128)}, f32[2,1,512]{2,1,0:T(1,128)S(1)}, u32[]{:S(2)}) copy-start(f32[2,1,512]{2,1,0:T(1,128)S(1)} %convert_element_type.199) | copy-start | bytes 12292
  15.2 117.3 %copy-start.32 = (f32[2,1,512]{2,1,0:T(1,128)}, f32[2,1,512]{2,1,0:T(1,128)S(1)}, u32[]{:S(2)}) copy-start(f32[2,1,512]{2,1,0:T(1,128)S(1)} %convert_element_type.200) | copy-start | bytes 12292
  27.3 105.3 %copy-start.3 = (bf16[1024,1024]{1,0:T(8,128)(2,1)S(1)}, bf16[1024,1024]{1,0:T(8,128)(2,1)}, u32[]{:S(2)}) copy-start(bf16[1024,1024]{1,0:T(8,128)(2,1)} %all-gather.13.cloned.1.call-done) | copy-start | bytes 6291460
  168.8 11.9 %copy-start.27 = (f32[8,512]{1,0:T(8,128)}, f32[8,512]{1,0:T(8,128)S(1)}, u32[]{:S(2)}) copy-start(f32[8,512]{1,0:T(8,128)S(1)} %fusion) | copy-start | bytes 49156
  224.2 12.0 %slice-start = ((s8[16777216]{0:T(1024)(128)(4,1)}), s8[4194304]{0:T(1024)(128)(4,1)S(1)}, s32[]{:S(2)}) async-start(s8[16777216]{0:T(1024)(128)(4,1)} %bitcast.108), calls=%async_computation.19 | async-start | bytes 8388608
  224.2 12.0 %slice-start.1 = ((s8[16777216]{0:T(1024)(128)(4,1)}), s8[4194304]{0:T(1024)(128)(4,1)S(1)}, s32[]{:S(2)}) async-start(s8[16777216]{0:T(1024)(128)(4,1)} %bitcast.108), calls=%async_computation.20 | async-start | bytes 8388608
  293.9 29.9 %copy-start.45 = (bf16[1024,2048]{1,0:T(8,128)(2,1)S(1)}, bf16[1024,2048]{1,0:T(8,128)(2,1)}, u32[]{:S(2)}) copy-start(bf16[1024,2048]{1,0:T(8,128)(2,1)} %all-gather.19.cloned.1.call-done) | copy-start | bytes 12582916
  329.6 212.8 %reduce-scatter.14.cloned.1.call-start = ((), (), s32[]{:S(2)}) async-start(), calls=%async_computation.16 | async-start | bytes 8912896 | tf_op jit(solution)/shard_map/reduce_scatter | solution.py:303
  329.8 11.0 %copy-start.17 = (bf16[1024,1024]{1,0:T(8,128)(2,1)S(1)}, bf16[1024,1024]{1,0:T(8,128)(2,1)}, u32[]{:S(2)}) copy-start(bf16[1024,1024]{1,0:T(8,128)(2,1)} %all-gather.23.cloned.1.call-done) | copy-start | bytes 6291460
  351.7 275.7 %reduce-scatter.10.cloned.1.call-start = ((), (), s32[]{:S(2)}) async-start(), calls=%async_computation.13 | async-start | bytes 2228224 | tf_op jit(solution)/shard_map/reduce_scatter | solution.py:291
  379.1 429.3 %reduce-scatter.12.cloned.1.call-start = ((), (), s32[]{:S(2)}) async-start(), calls=%async_computation.14 | async-start | bytes 8912896 | tf_op jit(solution)/shard_map/reduce_scatter | solution.py:297
  390.3 499.9 %reduce-scatter.6.cloned.1.call-start = ((), (), s32[]{:S(2)}) async-start(), calls=%async_computation.10 | async-start | bytes 3145728 | tf_op jit(solution)/shard_map/reduce_scatter | solution.py:205
  400.9 570.9 %reduce-scatter.8.cloned.1.call-start = ((), (), s32[]{:S(2)}) async-start(), calls=%async_computation.12 | async-start | bytes 6684672 | tf_op jit(solution)/shard_map/reduce_scatter | solution.py:285
  421.8 122.4 %copy-start.43 = (bf16[512]{0:T(512)(128)(2,1)S(1)}, bf16[512]{0:T(512)(128)(2,1)}, u32[]{:S(2)}) copy-start(bf16[512]{0:T(512)(128)(2,1)} %param.28) | copy-start | bytes 3076
  421.8 122.4 %copy-start.44 = (bf16[512]{0:T(512)(128)(2,1)S(1)}, bf16[512]{0:T(512)(128)(2,1)}, u32[]{:S(2)}) copy-start(bf16[512]{0:T(512)(128)(2,1)} %param.22) | copy-start | bytes 3076
  421.8 122.4 %copy-start.29 = (f32[8,3,64]{2,0,1:T(8,128)S(1)}, f32[8,3,64]{2,0,1:T(8,128)}, u32[]{:S(2)}) copy-start(f32[8,3,64]{2,0,1:T(8,128)} %get-tuple-element.113) | copy-start | bytes 18436
  421.8 220.2 %copy-start.5 = (bf16[1024,1024]{1,0:T(8,128)(2,1)S(1)}, bf16[1024,1024]{1,0:T(8,128)(2,1)}, u32[]{:S(2)}) copy-start(bf16[1024,1024]{1,0:T(8,128)(2,1)} %get-tuple-element.109) | copy-start | bytes 6291460
  421.8 578.4 %all-gather.27.cloned.1.call-start = ((), (), s32[]{:S(2)}) async-start(), calls=%async_computation.17 | async-start | bytes 1310720 | tf_op jit(solution)/shard_map/all_gather | solution.py:320
  544.2 485.0 %all-gather.25.cloned.1.call-start = ((), (), s32[]{:S(2)}) async-start(), calls=%async_computation.15 | async-start | bytes 1310720 | tf_op jit(solution)/shard_map/all_gather | solution.py:317
  642.0 168.2 %copy-start.11 = (bf16[1024,512]{1,0:T(8,128)(2,1)S(1)}, bf16[1024,512]{1,0:T(8,128)(2,1)}, u32[]{:S(2)}) copy-start(bf16[1024,512]{1,0:T(8,128)(2,1)} %param.29) | copy-start | bytes 3145732
  810.2 80.0 %copy-start.12 = (bf16[1024,512]{1,0:T(8,128)(2,1)S(1)}, bf16[1024,512]{1,0:T(8,128)(2,1)}, u32[]{:S(2)}) copy-start(bf16[1024,512]{1,0:T(8,128)(2,1)} %param.15) | copy-start | bytes 3145732
  890.2 141.8 %copy-start.38 = (f32[512]{0:T(512)}, f32[512]{0:T(512)S(1)}, u32[]{:S(2)}) copy-start(f32[512]{0:T(512)S(1)} %get-tuple-element.183) | copy-start | bytes 6148
  (34 other events, 156.4 us)
Sparse Core Ops, SparseCore 0:
  9.6 13.2 all-gather.12
  24.5 31.3 all-gather.16
  57.4 8.8 all-gather.22
  67.8 64.6 all-gather.14
  133.9 79.4 all-gather.18
  214.8 79.0 all-gather.20
  329.7 26.7 all-reduce.3
  358.9 183.4 reduce-scatter.13
  545.3 81.9 reduce-scatter.9
  629.6 178.7 reduce-scatter.11
  811.3 7.1 reduce-scatter.5
  823.6 148.2 reduce-scatter.7
  973.7 26.4 all-gather.26
  1002.5 26.6 all-gather.24
where the time goes:
time: 1050 us; the launch traced here: 1040 us
  waiting for transfers between devices  617 us (59%)
  matrix products  160 us (15%)
  blocking collectives  105 us (10%)
  other arithmetic  89 us (8%)
  local copies, waits for them, and re-layouts  52.8 us (5%)
  between operations  15.3 us (1%)
    reduce_scatter x1, waiting for transfers between devices, local(): lax.psum_scatter(regroup(grad_up_weight, 0, row_count, group_count), ('dp...  164 us
    reduce_scatter x1, waiting for transfers between devices, local(): lax.psum_scatter(regroup(grad_down_weight, 1, row_count, group_count), ('...  120 us
    reduce_scatter x1, waiting for transfers between devices, local(): lax.psum_scatter(regroup(grad_out_weight, 1, row_count, group_count), ('d...  83 us
    reduce_scatter x1, waiting for transfers between devices, local(): lax.psum_scatter(regroup(grad_qkv_weight, 0, row_count, group_count), ('d...  78.8 us
    psum x1, blocking collectives, local(): lax.psum((jnp.sum(grad_mixed.astype(jnp.float32), axis=0), jnp.sum(grad_u...  74.1 us
    all_gather x1, waiting for transfers between devices, local(): lax.all_gather(qkv_weight, 'row', axis=0, tiled=True)  62.1 us
    all_gather x1, waiting for transfers between devices, local(): lax.all_gather(out_weight, 'row', axis=1, tiled=True)  28.6 us
    dot_general x1, matrix products, local(): jnp.dot(cot_all, down_all.T, preferred_element_type=jnp.float32)  27.9 us
  transfers between devices with their start and end apart: 14, of which 10 were waited for; matrix products, arithmetic and copies ran while one was open for 24% of the time, Pallas kernels for 0%

commit v1 on v0

v1 whole, which is shorter than its diff:
```python
import functools

import jax
import jax.numpy as jnp
from jax import lax
from jax.experimental import pallas as pl
from jax.experimental.pallas import tpu as pltpu
from jax.sharding import PartitionSpec as P

HEAD_DIM = 64
ROT = 16
EPS = 1e-05
MAX_DOC = 512
LANES = 128
BF16 = jnp.bfloat16
F32 = jnp.float32

NT = (((1,), (1,)), ((), ()))
TN = (((0,), (0,)), ((), ()))
NN = (((1,), (0,)), ((), ()))


def dot(a, b, dims=NN):
    return lax.dot_general(a, b, dims, preferred_element_type=F32)


def doc_positions(segments):
    length = segments.shape[-1]
    places = jnp.arange(length, dtype=jnp.int32)
    changed = jnp.concatenate(
        [jnp.ones(segments.shape[:-1] + (1,), dtype=bool), segments[..., 1:] != segments[..., :-1]],
        axis=-1,
    )
    starts = lax.cummax(jnp.where(changed, places, jnp.zeros_like(places)), axis=segments.ndim - 1)
    return places - starts


def rotary_tables(positions):
    lane = jnp.arange(LANES) % HEAD_DIM
    frequency = 10000.0 ** (-2.0 * (lane % (ROT // 2)).astype(F32) / ROT)
    turning = lane < ROT
    angles = positions.astype(F32)[:, None] * jnp.where(turning, frequency, 0.0)[None, :]
    sign = jnp.where(turning, jnp.where(lane < ROT // 2, -1.0, 1.0), 0.0)
    return jnp.cos(angles), jnp.sin(angles) * sign[None, :]


def turn(values, cos_rows, sine_rows, low_lanes):
    half = ROT // 2
    up = pltpu.roll(values, values.shape[1] - half, 1)
    down = pltpu.roll(values, half, 1)
    return values * cos_rows + jnp.where(low_lanes, up, down) * sine_rows


def attention_kernel(
    q_ref, k_ref, v_ref, gc_ref, seg_row_ref, seg_col_ref, cos_ref, sin_ref, ctx_ref, gm_ref, dk_acc, dv_acc, *, block
):
    pair = pl.program_id(0)
    pairs = pl.num_programs(0)
    length = q_ref.shape[0]
    lane = lax.broadcasted_iota(jnp.int32, (1, LANES), 1)
    low_lanes = lane % HEAD_DIM < ROT // 2
    first = lane < HEAD_DIM
    zero = jnp.zeros((), BF16)

    def split(values):
        return [jnp.where(first, values, zero), jnp.where(first, zero, values)]

    dk_acc[...] = jnp.zeros_like(dk_acc)
    dv_acc[...] = jnp.zeros_like(dv_acc)
    for begin in range(0, length, block):
        low = max(0, begin - (MAX_DOC - 1)) // LANES * LANES
        rows = pl.ds(begin, block)
        keys = pl.ds(low, begin + block - low)
        width = begin + block - low
        q_parts = split(q_ref[rows, :] * jnp.asarray(HEAD_DIM**-0.5, BF16))
        g_parts = split(gc_ref[rows, :])
        k_block = k_ref[keys, :]
        v_block = v_ref[keys, :]
        places = begin + lax.broadcasted_iota(jnp.int32, (block, width), 0)
        key_places = low + lax.broadcasted_iota(jnp.int32, (block, width), 1)
        allowed = (seg_col_ref[rows, :] == seg_row_ref[:, keys]) & (places >= key_places)
        probs = []
        grads = []
        for part in range(2):
            scores = dot(q_parts[part], k_block, NT)
            scores = jnp.where(allowed, scores, -1e30)
            top = jnp.max(scores, axis=1, keepdims=True)
            powers = jnp.exp(scores - top)
            total = jnp.sum(powers, axis=1, keepdims=True)
            chances = powers * (1.0 / total)
            slopes = dot(g_parts[part], v_block, NT)
            inner = jnp.sum(slopes * chances, axis=1, keepdims=True)
            probs.append(chances.astype(BF16))
            grads.append((chances * (slopes - inner)).astype(BF16))
        context = jnp.where(first, dot(probs[0], v_block), dot(probs[1], v_block))
        ctx_ref[rows, :] = context.astype(BF16)
        dq = jnp.where(first, dot(grads[0], k_block), dot(grads[1], k_block)) * HEAD_DIM**-0.5
        dq = turn(dq, cos_ref[rows, :], -sin_ref[rows, :], low_lanes)
        gm_ref[rows, pl.ds(pl.multiple_of(pair * LANES, LANES), LANES)] = dq.astype(BF16)
        dk_acc[keys, :] += dot(grads[0], q_parts[0], TN) + dot(grads[1], q_parts[1], TN)
        dv_acc[keys, :] += dot(probs[0], g_parts[0], TN) + dot(probs[1], g_parts[1], TN)
    dk = turn(dk_acc[...], cos_ref[...], -sin_ref[...], low_lanes)
    gm_ref[:, pl.ds(pl.multiple_of((pairs + pair) * LANES, LANES), LANES)] = dk.astype(BF16)
    gm_ref[:, pl.ds(pl.multiple_of((2 * pairs + pair) * LANES, LANES), LANES)] = dv_acc[...].astype(BF16)


def attention(qkv, grad_context, seg_row, cos_rows, sine_rows):
    length, wide = qkv.shape
    pairs = wide // (3 * LANES)
    block = min(256, length)
    column = lambda shift: pl.BlockSpec((length, LANES), lambda p: (0, shift + p))
    whole = lambda *shape: pl.BlockSpec(shape, lambda p: (0, 0))
    flops = pairs * 2 * 6 * 2 * length * length * LANES // 2
    return pl.pallas_call(
        functools.partial(attention_kernel, block=block),
        grid=(pairs,),
        in_specs=[
            column(0),
            column(pairs),
            column(2 * pairs),
            column(0),
            whole(1, length),
            whole(length, 1),
            whole(length, LANES),
            whole(length, LANES),
        ],
        out_specs=[column(0), whole(length, wide)],
        out_shape=[
            jax.ShapeDtypeStruct((length, pairs * LANES), BF16),
            jax.ShapeDtypeStruct((length, wide), BF16),
        ],
        scratch_shapes=[pltpu.VMEM((length, LANES), F32), pltpu.VMEM((length, LANES), F32)],
        compiler_params=pltpu.CompilerParams(vmem_limit_bytes=48 << 20),
        cost_estimate=pl.CostEstimate(
            flops=flops, bytes_accessed=6 * length * wide, transcendentals=pairs * length * length
        ),
        name="attention",
    )(qkv, qkv, qkv, grad_context, seg_row, seg_row.reshape(length, 1), cos_rows, sine_rows)


def feed_kernel(a_ref, g_ref, up_ref, bias_ref, down_ref, act_ref, gup_ref, sum_ref, *, chunk):
    units = up_ref.shape[1]

    @pl.when(pl.program_id(0) == 0)
    def _():
        sum_ref[...] = jnp.zeros_like(sum_ref)

    for begin in range(0, units, chunk):
        cols = pl.ds(begin, chunk)
        up = dot(a_ref[...], up_ref[:, cols]) + bias_ref[:, cols]
        pull = dot(g_ref[...], down_ref[cols, :], NT)
        gate = 0.5 * (1.0 + lax.erf(up * 0.5**0.5))
        bell = jnp.exp(-0.5 * up * up) * 0.3989422804014327
        act_ref[:, cols] = (up * gate).astype(BF16)
        grad = (pull * (gate + up * bell)).astype(BF16)
        gup_ref[:, cols] = grad
        sum_ref[:, cols] += jnp.sum(grad.astype(F32), axis=0, keepdims=True)


def feed(normed, cot, up_weight, up_bias, down_weight):
    tokens, width = normed.shape
    units = up_weight.shape[1]
    block = min(256, tokens)
    rows = lambda size: pl.BlockSpec((block, size), lambda i: (i, 0))
    whole = lambda *shape: pl.BlockSpec(shape, lambda i: (0, 0))
    return pl.pallas_call(
        functools.partial(feed_kernel, chunk=min(256, units)),
        grid=(tokens // block,),
        in_specs=[rows(width), rows(width), whole(width, units), whole(1, units), whole(units, width)],
        out_specs=[rows(units), rows(units), whole(1, units)],
        out_shape=[
            jax.ShapeDtypeStruct((tokens, units), BF16),
            jax.ShapeDtypeStruct((tokens, units), BF16),
            jax.ShapeDtypeStruct((1, units), F32),
        ],
        compiler_params=pltpu.CompilerParams(vmem_limit_bytes=48 << 20),
        cost_estimate=pl.CostEstimate(
            flops=4 * tokens * width * units,
            bytes_accessed=4 * tokens * width + 4 * width * units + 4 * tokens * units,
            transcendentals=2 * tokens * units,
        ),
        name="feed",
    )(normed, cot, up_weight, up_bias, down_weight)


def normalize(values):
    centred = values - jnp.mean(values, axis=-1, keepdims=True)
    variance = jnp.mean(centred * centred, axis=-1, keepdims=True)
    inv_std = lax.rsqrt(variance + EPS)
    return centred * inv_std, inv_std


def make_local(groups, rows, cols):
    quarters = groups // 2

    def pair_swap(value):
        return lax.ppermute(value, "dp", [(d, d ^ 1) for d in range(groups)])

    def quarter_shift(value, shift):
        moves = [(2 * a + b, 2 * ((a + shift) % quarters) + b) for a in range(quarters) for b in range(2)]
        return lax.ppermute(value, "dp", moves)

    def row_shift(value, shift):
        return lax.ppermute(value, "row", [(r, (r + shift) % rows) for r in range(rows)])

    def core_swap(value):
        return lax.ppermute(value, "col", [(0, 1), (1, 0)])

    def local(
        hidden,
        segments,
        ln1_gain,
        ln1_bias,
        qkv_weight,
        qkv_bias,
        out_weight,
        out_bias,
        ln2_gain,
        ln2_bias,
        up_weight,
        up_bias,
        down_weight,
        down_bias,
        cotangent,
    ):
        assert segments.shape[0] == 1 and cols == 2
        length = segments.shape[1]
        half_width = hidden.shape[1]
        width = 2 * half_width
        shard = qkv_weight.shape[0]
        heads = qkv_weight.shape[1] // (3 * HEAD_DIM) // 2
        wide = heads * HEAD_DIM
        units = up_weight.shape[1] // 2
        whole_heads = heads % quarters == 0
        dp = lax.axis_index("dp")
        row = lax.axis_index("row")
        col = lax.axis_index("col")
        side = lax.rem(dp, 2)
        quarter = dp // 2

        def both(mine, other):
            flip = col == 0
            return jnp.concatenate([jnp.where(flip, mine, other), jnp.where(flip, other, mine)], axis=-1)

        def half_of(value, axis):
            size = value.shape[axis] // 2
            return lax.dynamic_slice_in_dim(value, side * size, size, axis)

        def piece_of(value, shift, axis, placed=False):
            size = value.shape[axis] // quarters
            if placed:
                return lax.slice_in_dim(value, shift * size, (shift + 1) * size, axis=axis)
            return lax.dynamic_slice_in_dim(value, lax.rem(quarter - shift + quarters, quarters) * size, size, axis)

        def in_place(pieces, axis):
            if quarters == 1:
                return pieces[0]
            if quarters == 2:
                flip = quarter == 0
                first = jnp.where(flip, pieces[0], pieces[1])
                second = jnp.where(flip, pieces[1], pieces[0])
                return jnp.concatenate([first, second], axis=axis)
            order = lax.rem(quarter - jnp.arange(quarters) + quarters, quarters)
            stacked = jnp.take(jnp.stack(pieces), order, axis=0)
            return jnp.concatenate([stacked[i] for i in range(quarters)], axis=axis)

        def near(pieces, axis, keep):
            return jnp.concatenate(pieces, axis=axis) if keep else in_place(pieces, axis)

        def gather(value, width_axis, unit_axis, keep):
            mine = piece_of(value, 0, unit_axis)
            received = {0: mine}
            ahead = behind = mine
            for step in range(1, rows):
                if step <= rows // 2:
                    ahead = row_shift(ahead, -1)
                    received[step] = ahead
                if step <= (rows - 1) // 2:
                    behind = row_shift(behind, 1)
                    received[rows - step] = behind
            result = jnp.zeros(
                [width if i == width_axis else n for i, n in enumerate(value.shape)], value.dtype
            )
            for step in range(rows):
                if step == 0:
                    pieces = [piece_of(value, q, unit_axis) for q in range(quarters)]
                else:
                    pieces = [received[step]]
                    pieces += [quarter_shift(received[step], q) for q in range(1, quarters)]
                block = near(pieces, unit_axis, keep)
                place = lax.rem(row + step, rows) * shard
                result = lax.dynamic_update_slice_in_dim(result, block, place, width_axis)
            return result

        hidden_other = core_swap(hidden)
        hidden_far = pair_swap(hidden)
        cot_other = core_swap(cotangent)
        cot_far = pair_swap(cotangent)
        params = jnp.stack([ln1_gain, ln1_bias, ln2_gain, ln2_bias])
        params = both(params, core_swap(params)).astype(F32)
        gain_one, shift_one, gain_two, shift_two = [params[i][None, :] for i in range(4)]
        inputs = [both(hidden, hidden_other), both(hidden_far, core_swap(hidden_far))]
        cots = [both(cotangent, cot_other), both(cot_far, core_swap(cot_far))]
        segs = [segments, pair_swap(segments)]

        qkv_cols = qkv_weight.reshape(shard, 2, heads, 3, HEAD_DIM)
        qkv_cols = lax.dynamic_index_in_dim(qkv_cols, side, 1, keepdims=False)
        qkv_cols = jnp.swapaxes(qkv_cols, 1, 2).reshape(shard, 3, wide)
        qkv_all = gather(qkv_cols, 0, 2, whole_heads).reshape(width, 3 * wide)
        out_all = gather(half_of(out_weight, 0), 1, 0, whole_heads)
        up_all = gather(half_of(up_weight, 1), 0, 1, True)
        down_all = gather(half_of(down_weight, 0), 1, 0, True)

        bias_cols = lax.dynamic_index_in_dim(qkv_bias.reshape(2, heads, 3, HEAD_DIM), side, 0, keepdims=False)
        bias_cols = jnp.swapaxes(bias_cols, 0, 1).reshape(1, 3, wide)
        bias_cols = near([piece_of(bias_cols, q, 2) for q in range(quarters)], 2, whole_heads)
        bias_cols = bias_cols.reshape(1, 3 * wide).astype(F32)
        up_half = half_of(up_bias, 0)
        up_row = jnp.concatenate([piece_of(up_half, q, 0) for q in range(quarters)])[None, :].astype(F32)

        norms = []
        contexts = []
        grads_mixed = []
        for values, cot, seg in zip(inputs, cots, segs):
            unit, inv = normalize(values.astype(F32))
            act_one = (unit * gain_one + shift_one).astype(BF16)
            act_two = (unit * gain_two + shift_two).astype(BF16)
            norms.append((unit, inv, act_one, act_two))
            cos_rows, sine_rows = rotary_tables(doc_positions(seg).reshape(length))
            mixed = dot(act_one, qkv_all) + bias_cols
            cos_wide = jnp.tile(cos_rows, (1, 2 * wide // LANES))
            sine_wide = jnp.tile(sine_rows, (1, 2 * wide // LANES))
            turned = mixed[:, : 2 * wide]
            lane = jnp.arange(2 * wide) % HEAD_DIM
            swapped = jnp.where(
                lane < ROT // 2, jnp.roll(turned, -(ROT // 2), axis=1), jnp.roll(turned, ROT // 2, axis=1)
            )
            turned = turned * cos_wide + swapped * sine_wide
            qkv = jnp.concatenate([turned, mixed[:, 2 * wide :]], axis=1).astype(BF16)
            grad_context = dot(cot, out_all, NT).astype(BF16)
            context, grad_mixed = attention(qkv, grad_context, seg, cos_rows, sine_rows)
            contexts.append(context)
            grads_mixed.append(grad_mixed)

        feeds = [feed(norm[3], cot, up_all, up_row, down_all) for norm, cot in zip(norms, cots)]

        def reduce_grad(left, right, width_axis, unit_axis, placed, shape=None):
            total = dot(left[0], right[0], TN) + dot(left[1], right[1], TN)
            if shape is not None:
                total = total.reshape(shape)
            mine = piece_of(total, 0, unit_axis, placed)
            for q in range(1, quarters):
                part = piece_of(total, q, unit_axis, placed).astype(BF16)
                mine = mine + quarter_shift(part, -q).astype(F32)
            cut = lambda t: lax.dynamic_slice_in_dim(mine, lax.rem(row + t, rows) * shard, shard, width_axis)
            result = cut(0)
            for t in range(1, rows):
                result = result + row_shift(cut(t).astype(BF16), t).astype(F32)
            result = result.astype(BF16)
            pieces = [result] + [quarter_shift(result, q) for q in range(1, quarters)]
            result = in_place(pieces, unit_axis)
            far = pair_swap(result)
            flip = side == 0
            return jnp.concatenate(
                [jnp.where(flip, result, far), jnp.where(flip, far, result)], axis=unit_axis
            ).astype(F32)

        acts_one = [n[2] for n in norms]
        acts_two = [n[3] for n in norms]
        out_grad = reduce_grad(contexts, cots, 1, 0, whole_heads)
        qkv_grad = reduce_grad(acts_one, grads_mixed, 0, 2, whole_heads, (width, 3, wide))
        down_grad = reduce_grad([f[0] for f in feeds], cots, 1, 0, True)
        up_grad = reduce_grad(acts_two, [f[1] for f in feeds], 0, 1, True)
        qkv_grad = qkv_grad.reshape(shard, 3, 2 * heads, HEAD_DIM)
        qkv_grad = jnp.swapaxes(qkv_grad, 1, 2).reshape(shard, 6 * wide)

        outs = []
        slopes = []
        norm_sums = jnp.zeros((4, width), F32)
        for index in range(2):
            unit, inv, _, _ = norms[index]
            act, grad_up, _ = feeds[index]
            outs.append((dot(contexts[index], out_all) + dot(act, down_all)).astype(BF16))
            grad_one = dot(grads_mixed[index], qkv_all, NT)
            grad_two = dot(grad_up, up_all, NT)
            norm_sums += jnp.stack(
                [
                    jnp.sum(grad_one * unit, axis=0),
                    jnp.sum(grad_one, axis=0),
                    jnp.sum(grad_two * unit, axis=0),
                    jnp.sum(grad_two, axis=0),
                ]
            )
            scaled = grad_one * gain_one + grad_two * gain_two
            mean_scaled = jnp.mean(scaled, axis=1, keepdims=True)
            mean_unit = jnp.mean(scaled * unit, axis=1, keepdims=True)
            slopes.append((inv * (scaled - mean_scaled - unit * mean_unit)).astype(BF16))

        def fold(pair):
            sums = []
            for value in pair:
                kept = lax.dynamic_slice_in_dim(value, col * half_width, half_width, 1).astype(F32)
                given = lax.dynamic_slice_in_dim(value, (1 - col) * half_width, half_width, 1)
                sums.append(kept + core_swap(given).astype(F32))
            return sums[0] + pair_swap(sums[1].astype(BF16)).astype(F32)

        cot_local = cotangent.astype(F32)
        output = hidden.astype(F32) + fold(outs) + (out_bias.astype(F32) + down_bias.astype(F32))
        input_grad = cot_local + fold(slopes)

        qkv_sum = (
            jnp.sum(grads_mixed[0].astype(F32), axis=0) + jnp.sum(grads_mixed[1].astype(F32), axis=0)
        ).reshape(3, wide)
        if whole_heads:
            qkv_sum = in_place([piece_of(qkv_sum, q, 1, True) for q in range(quarters)], 1)
        up_sum = (feeds[0][2] + feeds[1][2])[0]
        up_sum = in_place([piece_of(up_sum, q, 0, True) for q in range(quarters)], 0)

        def widen(value):
            zeros = jnp.zeros_like(value)
            flip = side == 0
            return jnp.concatenate([jnp.where(flip, value, zeros), jnp.where(flip, zeros, value)], axis=-1)

        kept = lax.dynamic_slice_in_dim(norm_sums, col * half_width, half_width, 1)
        given = lax.dynamic_slice_in_dim(norm_sums, (1 - col) * half_width, half_width, 1)
        norm_sums = kept + core_swap(given)
        small = jnp.concatenate(
            [widen(qkv_sum).reshape(-1), widen(up_sum), jnp.sum(cot_local, axis=0), norm_sums.reshape(-1)]
        )
        small = lax.psum(small, ("dp", "row"))
        sizes = [6 * wide, 2 * units, half_width, half_width, half_width, half_width, half_width]
        parts = []
        start = 0
        for size in sizes:
            parts.append(lax.slice_in_dim(small, start, start + size))
            start += size
        qkv_sum, up_sum, cot_sum, gain_one_sum, shift_one_sum, gain_two_sum, shift_two_sum = parts
        qkv_sum = jnp.swapaxes(qkv_sum.reshape(3, 2 * heads, HEAD_DIM), 0, 1).reshape(-1)
        return (
            output,
            input_grad,
            gain_one_sum,
            shift_one_sum,
            qkv_grad,
            qkv_sum,
            out_grad,
            cot_sum,
            gain_two_sum,
            shift_two_sum,
            up_grad,
            up_sum,
            down_grad,
            cot_sum,
        )

    return local


def solution(mesh):
    placed = (
        P(("dp", "row"), "col"),
        P(("dp", "row"), None),
        P("col"),
        P("col"),
        P("row", "col"),
        P("col"),
        P("col", "row"),
        P("col"),
        P("col"),
        P("col"),
        P("row", "col"),
        P("col"),
        P("col", "row"),
        P("col"),
        P(("dp", "row"), "col"),
    )
    return jax.shard_map(
        make_local(mesh.shape["dp"], mesh.shape["row"], mesh.shape["col"]),
        mesh=mesh,
        in_specs=placed,
        out_specs=(
            P(("dp", "row"), "col"),
            P(("dp", "row"), "col"),
            P("col"),
            P("col"),
            P("row", "col"),
            P("col"),
            P("col", "row"),
            P("col"),
            P("col"),
            P("col"),
            P("row", "col"),
            P("col"),
            P("col", "row"),
            P("col"),
        ),
        check_vma=False,
    )
```

time: 1050 us -> 571 us (0.54)
  waiting for transfers between devices: 617 us -> 192 us
  matrix products: 160 us -> 68.9 us
  starting transfers between devices: 1.02 us -> 83.2 us
  Pallas kernels: 0 us -> 42.3 us
  blocking collectives: 105 us -> 72.2 us
  other arithmetic: 89 us -> 61.6 us
  between operations: 15.3 us -> 2.5 us
  local copies, waits for them, and re-layouts: 52.8 us -> 40.9 us
    reduce_scatter x5 -> x0, waiting for transfers between devices: 446 us -> none  [the longest x1 164 us: local(): lax.psum_scatter(regroup(grad_up_weight, 0, row_count, group_count), ('dp...]
    ppermute x0 -> x63, waiting for transfers between devices: none -> 192 us  [the longest x20 79.7 us: quarter_shift(): return lax.ppermute(value, 'dp', moves)]
    all_gather x8 -> x0, waiting for transfers between devices: 167 us -> none  [the longest x1 62.1 us: local(): lax.all_gather(qkv_weight, 'row', axis=0, tiled=True)]
    dot_general x24 -> x20, matrix products: 160 us -> 68.9 us  [dot(): return lax.dot_general(a, b, dims, preferred_element_type=F32)]
    ppermute x0 -> x63, starting transfers between devices: none -> 83.2 us  [the longest x24 53 us: row_shift(): lax.ppermute(value, 'row', [(r, (r + shift) % rows) for r in range(rows)])]
    pallas_call x0 -> x4, Pallas kernels: none -> 42.3 us  [the longest x2 24.2 us: attention(): pl.pallas_call(functools.partial(attention_kernel, block=block), grid=(pa...]
    convert_element_type x18 -> x17, other arithmetic: 52.4 us -> 14.1 us  [the longest x3 3.51 us: reduce_grad(): return jnp.concatenate([jnp.where(flip, result, far), jnp.where(flip, far...]
    all_gather x6 -> x0, blocking collectives: 30.4 us -> none  [the longest x1 14.4 us: local(): lax.all_gather(piece_qkv.astype(jnp.bfloat16), 'dp', axis=0, tiled=True)]
  transfers between devices with their start and end apart: 14 -> 63, of which waited for: 10 -> 24; matrix products, arithmetic and copies ran while one was open for 24% -> 15% of each run, Pallas kernels for 0% -> 0%
where the time goes in v1:
time: 571 us; the launch traced here: 564 us
  waiting for transfers between devices  192 us (34%)
  starting transfers between devices  83.2 us (15%)
  blocking collectives  72.2 us (13%)
  matrix products  68.9 us (12%)
  other arithmetic  61.6 us (11%)
  Pallas kernels  42.3 us (7%)
  local copies, waits for them, and re-layouts  40.9 us (7%)
    ppermute x20, waiting for transfers between devices, quarter_shift(): return lax.ppermute(value, 'dp', moves)  79.7 us
    psum x1, blocking collectives, local(): small = lax.psum(small, ('dp', 'row'))  72.2 us
    dot_general x20, matrix products, dot(): return lax.dot_general(a, b, dims, preferred_element_type=F32)  68.9 us
    ppermute x9, waiting for transfers between devices, pair_swap(): return lax.ppermute(value, 'dp', [(d, d ^ 1) for d in range(groups)])  61.6 us
    ppermute x24, starting transfers between devices, row_shift(): lax.ppermute(value, 'row', [(r, (r + shift) % rows) for r in range(rows)])  53 us
    ppermute x24, waiting for transfers between devices, row_shift(): lax.ppermute(value, 'row', [(r, (r + shift) % rows) for r in range(rows)])  50.9 us
    pallas_call x2, Pallas kernels, attention(): pl.pallas_call(functools.partial(attention_kernel, block=block), grid=(pa...  24.2 us
    ppermute x20, starting transfers between devices, quarter_shift(): return lax.ppermute(value, 'dp', moves)  20.4 us
  transfers between devices with their start and end apart: 63, of which 24 were waited for; matrix products, arithmetic and copies ran while one was open for 15% of the time, Pallas kernels for 0%

profile of v1, /device:TPU:0, one launch (start us, length us, event | category | flops | bytes accessed | tf_op | source)
XLA Modules:
  0.0 563.8 jit_solution(16195697617211666627)
XLA Ops:
  3.1 5.0 collective-permute-start.2
  28.4 4.4 multiply_cosine_fusion
  52.0 5.2 collective-permute-done.15
  63.0 4.4 collective-permute-start.17
  97.2 4.8 collective-permute-done.26
  111.5 20.8 %collective-permute-done.31 = bf16[1024,512]{1,0:T(8,128)(2,1)S(1)} collective-permute-done((bf16[1024,512]{1,0:T(8,128)(2,1)S(1)}, bf16[1024,512]{1,0:T(8,128)(2,1)S(1)}, u32[]{:S(2)}, u32[]{:S(2)}) %collective-permute-start.31) | collective-permute-done | bytes 1048608 | tf_op jit(solution)/shard_map/ppermute | solution.py:197
  150.5 5.4 fusion.41
  157.2 11.9 %attention.3 = (bf16[1024,256]{1,0:T(8,128)(2,1)S(1)}, bf16[1024,768]{1,0:T(8,128)(2,1)S(1)}) custom-call(bf16[1024,768]{1,0:T(8,128)(2,1)S(1)} %pad_maximum_fusion.5.q_ref.k_ref.v_ref, bf16[1024,768]{1,0:T(8,128)(2,1)S(1)} %pad_maximum_fusion.5.q_ref.k_ref.v_ref, bf16[1024,768]{1,0:T(8,128)(2,1)S(1)} %pad_maximum_fusion.5.q_ref.k_ref.v_ref, ...), custom_call_target="tpu_custom_call" | custom-call | flops 3221225472 | bytes 4718592 | tf_op jit(solution)/shard_map/attention/pallas_call | solution.py:114
  180.4 9.1 %feed.2 = (bf16[1024,1024]{1,0:T(8,128)(2,1)S(1)}, bf16[1024,1024]{1,0:T(8,128)(2,1)S(1)}, f32[1,1024]{1,0:T(1,128)S(1)}) custom-call(bf16[1024,1024]{1,0:T(8,128)(2,1)} %get-tuple-element.168.a_ref, bf16[1024,1024]{1,0:T(8,128)(2,1)} %pad_maximum_fusion.1.g_ref, bf16[1024,1024]{1,0:T(8,128)(2,1)} %maximum_dynamic-update-slice_fusion.3.up_ref, ...), custom_call_target="tpu_custom_call" | custom-call | flops 4294967296 | bytes 12582912 | tf_op jit(solution)/shard_map/feed/pallas_call | solution.py:166
  189.6 6.1 %fusion.88 = f32[1024,1024]{1,0:T(8,128)} fusion(bf16[1024,1024]{1,0:T(8,128)(2,1)S(1)} %get-tuple-element.29, bf16[1024,1024]{1,0:T(8,128)(2,1)} %maximum_dynamic-update-slice_fusion.3.up_ref), kind=kOutput, calls=%fused_computation.260 | convolution fusion | flops 2147483648 | bytes 8388608 | tf_op jit(solution)/shard_map/dot_general | solution.py:24
  195.7 4.4 fusion.91
  200.0 4.4 fusion.86
  204.5 4.3 fusion.75
  210.3 12.3 %attention.2 = (bf16[1024,256]{1,0:T(8,128)(2,1)S(1)}, bf16[1024,768]{1,0:T(8,128)(2,1)S(1)}) custom-call(bf16[1024,768]{1,0:T(8,128)(2,1)S(1)} %pad_maximum_fusion.4.q_ref.k_ref.v_ref, bf16[1024,768]{1,0:T(8,128)(2,1)S(1)} %pad_maximum_fusion.4.q_ref.k_ref.v_ref, bf16[1024,768]{1,0:T(8,128)(2,1)S(1)} %pad_maximum_fusion.4.q_ref.k_ref.v_ref, ...), custom_call_target="tpu_custom_call" | custom-call | flops 3221225472 | bytes 4718592 | tf_op jit(solution)/shard_map/attention/pallas_call | solution.py:114
  228.3 9.0 %feed.3 = (bf16[1024,1024]{1,0:T(8,128)(2,1)S(1)}, bf16[1024,1024]{1,0:T(8,128)(2,1)S(1)}, f32[1,1024]{1,0:T(1,128)S(1)}) custom-call(bf16[1024,1024]{1,0:T(8,128)(2,1)} %get-tuple-element.169.a_ref, bf16[1024,1024]{1,0:T(8,128)(2,1)} %pad_maximum_fusion.3.g_ref, bf16[1024,1024]{1,0:T(8,128)(2,1)} %maximum_dynamic-update-slice_fusion.3.up_ref, ...), custom_call_target="tpu_custom_call" | custom-call | flops 4294967296 | bytes 12582912 | tf_op jit(solution)/shard_map/feed/pallas_call | solution.py:166
  237.3 5.4 add_convert_fusion
  246.5 4.3 fusion.90
  251.2 10.0 %fusion.77 = (f32[1024]{0:T(1024)S(1)}, f32[1024]{0:T(1024)S(1)}, f32[1024]{0:T(1024)S(1)}, f32[1024]{0:T(1024)S(1)}, f32[1024]{0:T(1024)S(1)}, /*index=5*/f32[1...) fusion(f32[1024]{0:T(1024)S(1)} %add_rsqrt_fusion.1, ...), kind=kOutput, calls=%fused_computation.249 | convolution fusion | flops 1648349184 | bytes 28385280 | tf_op jit(solution)/shard_map/dot_general | solution.py:24
  265.9 4.7 fusion.67
  282.4 13.9 %collective-permute-done.45 = bf16[128,1024]{1,0:T(8,128)(2,1)S(1)} collective-permute-done((bf16[128,1024]{1,0:T(8,128)(2,1)S(1)}, bf16[128,1024]{1,0:T(8,128)(2,1)S(1)}, u32[]{:S(2)}, u32[]{:S(2)}) %collective-permute-start.45) | collective-permute-done | bytes 262176 | tf_op jit(solution)/shard_map/ppermute | solution.py:201
  296.4 4.2 collective-permute-start.48
  309.1 41.1 %collective-permute-done.49 = bf16[128,256]{1,0:T(8,128)(2,1)S(1)} collective-permute-done((bf16[128,256]{1,0:T(8,128)(2,1)S(1)}, bf16[128,256]{1,0:T(8,128)(2,1)S(1)}, u32[]{:S(2)}, u32[]{:S(2)}) %collective-permute-start.49) | collective-permute-done | bytes 65568 | tf_op jit(solution)/shard_map/ppermute | solution.py:201
  351.2 4.1 collective-permute-start.42
  360.6 9.1 %collective-permute-done.41 = bf16[256,3,128]{0,2,1:T(8,128)(2,1)S(1)} collective-permute-done((bf16[256,3,128]{0,2,1:T(8,128)(2,1)S(1)}, bf16[256,3,128]{0,2,1:T(8,128)(2,1)S(1)}, u32[]{:S(2)}, u32[]{:S(2)}) %collective-permute-start.41) | collective-permute-done | bytes 196640 | tf_op jit(solution)/shard_map/ppermute | solution.py:204
  381.6 8.7 %collective-permute-start.58 = (bf16[512,256]{1,0:T(8,128)(2,1)S(1)}, bf16[512,256]{1,0:T(8,128)(2,1)S(1)}, u32[]{:S(2)}, u32[]{:S(2)}) collective-permute-start(bf16[512,256]{1,0:T(8,128)(2,1)S(1)} %get-tuple-element.106), channel_id=1, source_target_pairs={{0,2},{2,4},{4,6},{6,0},{1,3},{3,5},{5,7},{7,1},{8,10},{10,12},{12... | collective-permute-start | bytes 786440 | tf_op jit(solution)/shard_map/ppermute | solution.py:204
  390.4 17.7 %collective-permute-done.53 = bf16[256,512]{0,1:T(8,128)(2,1)S(1)} collective-permute-done((bf16[256,512]{0,1:T(8,128)(2,1)S(1)}, bf16[256,512]{0,1:T(8,128)(2,1)S(1)}, u32[]{:S(2)}, u32[]{:S(2)}) %collective-permute-start.53) | collective-permute-done | bytes 262176 | tf_op jit(solution)/shard_map/ppermute | solution.py:204
  410.1 7.3 %collective-permute-done.59 = bf16[512,256]{1,0:T(8,128)(2,1)S(1)} collective-permute-done((bf16[512,256]{1,0:T(8,128)(2,1)S(1)}, bf16[512,256]{1,0:T(8,128)(2,1)S(1)}, u32[]{:S(2)}, u32[]{:S(2)}) %collective-permute-start.59) | collective-permute-done | bytes 262176 | tf_op jit(solution)/shard_map/ppermute | solution.py:204
  423.6 4.0 collective-permute-done.55
  429.2 5.1 collective-permute-done.61
  437.2 29.1 %collective-permute-done.37 = bf16[1024,512]{1,0:T(8,128)(2,1)} collective-permute-done((bf16[1024,512]{1,0:T(8,128)(2,1)}, bf16[1024,512]{1,0:T(8,128)(2,1)}, u32[]{:S(2)}, u32[]{:S(2)}) %collective-permute-start.37) | collective-permute-done | bytes 1048608 | tf_op jit(solution)/shard_map/ppermute | solution.py:197
  469.7 7.7 %collective-permute-done.56 = bf16[256,1024]{0,1:T(8,128)(2,1)S(1)} collective-permute-done((bf16[256,1024]{0,1:T(8,128)(2,1)S(1)}, bf16[256,1024]{0,1:T(8,128)(2,1)S(1)}, u32[]{:S(2)}, u32[]{:S(2)}) %collective-permute-start.56) | collective-permute-done | bytes 524320 | tf_op jit(solution)/shard_map/ppermute | solution.py:197
  478.4 72.2 %psum.7 = f32[6144]{0:T(1024)S(1)} all-reduce(f32[6144]{0:T(1024)S(1)} %constant_dynamic-update-slice_fusion), channel_id=1, replica_groups=mesh['dp'=4,'row'=4,'col'=2] {'dp','row'}, use_global_device_ids=true, to_apply=%region_23.24 | all-reduce | flops 6144 | bytes 49152 | tf_op jit(solution)/shard_map/psum | solution.py:430
  (462 shorter events, 201.0 us)
Async XLA Ops:
  3.1 47.2 %collective-permute-start.2 = (bf16[256,3,128]{0,2,1:T(8,128)(2,1)}, bf16[256,3,128]{0,2,1:T(8,128)(2,1)}, u32[]{:S(2)}, u32[]{:S(2)}) collective-permute-start(bf16[256,3,128]{0,2,1:T(8,128)(2,1)} %get-tuple-element.144), channel_id=1, source_target_pairs={{0,6},{2,0},{4,2},{6,4},{1,7},{3,1},{5,3},{7,5},{8,14},{10,8},{12,... | collective-permute-start | bytes 589832 | tf_op jit(solution)/shard_map/ppermute | solution.py:204
  8.1 43.8 %collective-permute-start.6 = (bf16[256,3,128]{0,2,1:T(8,128)(2,1)}, bf16[256,3,128]{0,2,1:T(8,128)(2,1)}, u32[]{:S(2)}, u32[]{:S(2)}) collective-permute-start(bf16[256,3,128]{0,2,1:T(8,128)(2,1)} %get-tuple-element.144), channel_id=1, source_target_pairs={{0,2},{2,4},{4,6},{6,0},{1,3},{3,5},{5,7},{7,1},{8,10},{10,12},{12... | collective-permute-start | bytes 589832 | tf_op jit(solution)/shard_map/ppermute | solution.py:204
  8.2 24.7 %collective-permute-start.9 = (bf16[128,256]{1,0:T(8,128)(2,1)S(1)}, bf16[128,256]{1,0:T(8,128)(2,1)}, u32[]{:S(2)}, u32[]{:S(2)}) collective-permute-start(bf16[128,256]{1,0:T(8,128)(2,1)S(1)} %get-tuple-element.148), channel_id=1, source_target_pairs={{0,6},{2,0},{4,2},{6,4},{1,7},{3,1},{5,3},{7,5},{8,14},{10,8},{12,... | collective-permute-start | bytes 196616 | tf_op jit(solution)/shard_map/ppermute | solution.py:204
  12.1 27.0 %collective-permute-start.13 = (bf16[128,256]{1,0:T(8,128)(2,1)S(1)}, bf16[128,256]{1,0:T(8,128)(2,1)S(1)}, u32[]{:S(2)}, u32[]{:S(2)}) collective-permute-start(bf16[128,256]{1,0:T(8,128)(2,1)S(1)} %get-tuple-element.148), channel_id=1, source_target_pairs={{0,2},{2,4},{4,6},{6,0},{1,3},{3,5},{5,7},{7,1},{8,10},{10,12},{12... | collective-permute-start | bytes 196616 | tf_op jit(solution)/shard_map/ppermute | solution.py:204
  44.8 15.4 %collective-permute-start.19 = (bf16[256,512]{1,0:T(8,128)(2,1)}, bf16[256,512]{1,0:T(8,128)(2,1)}, u32[]{:S(2)}, u32[]{:S(2)}) collective-permute-start(bf16[256,512]{1,0:T(8,128)(2,1)} %copy-done.55), channel_id=1, source_target_pairs={{0,2},{2,4},{4,6},{6,0},{1,3},{3,5},{5,7},{7,1},{8,10},{10,12},{12... | collective-permute-start | bytes 786440 | tf_op jit(solution)/shard_map/ppermute | solution.py:204
  44.8 18.2 %collective-permute-start.21 = (bf16[512,256]{1,0:T(8,128)(2,1)S(1)}, bf16[512,256]{1,0:T(8,128)(2,1)}, u32[]{:S(2)}, u32[]{:S(2)}) collective-permute-start(bf16[512,256]{1,0:T(8,128)(2,1)S(1)} %get-tuple-element.129), channel_id=1, source_target_pairs={{0,6},{2,0},{4,2},{6,4},{1,7},{3,1},{5,3},{7,5},{8,14},{10,8},{12,... | collective-permute-start | bytes 786440 | tf_op jit(solution)/shard_map/ppermute | solution.py:204
  50.3 17.1 %collective-permute-start.3 = (bf16[256,3,128]{0,2,1:T(8,128)(2,1)}, bf16[256,3,128]{0,2,1:T(8,128)(2,1)S(1)}, u32[]{:S(2)}, u32[]{:S(2)}) collective-permute-start(bf16[256,3,128]{0,2,1:T(8,128)(2,1)} %collective-permute-done.2), channel_id=1, source_target_pairs={{0,16},{8,24},{16,0},{24,8},{1,17},{9,25},{17,1},{25,9},{2,18},{10... | collective-permute-start | bytes 589832 | tf_op jit(solution)/shard_map/ppermute | solution.py:201
  52.0 16.0 %collective-permute-start.4 = (bf16[256,3,128]{0,2,1:T(8,128)(2,1)}, bf16[256,3,128]{0,2,1:T(8,128)(2,1)S(1)}, u32[]{:S(2)}, u32[]{:S(2)}) collective-permute-start(bf16[256,3,128]{0,2,1:T(8,128)(2,1)} %collective-permute-done.2), channel_id=1, source_target_pairs={{0,6},{2,0},{4,2},{6,4},{1,7},{3,1},{5,3},{7,5},{8,14},{10,8},{12,... | collective-permute-start | bytes 589832 | tf_op jit(solution)/shard_map/ppermute | solution.py:204
  68.0 34.2 %collective-permute-start = (bf16[1024,512]{1,0:T(8,128)(2,1)}, bf16[1024,512]{1,0:T(8,128)(2,1)S(1)}, u32[]{:S(2)}, u32[]{:S(2)}) collective-permute-start(bf16[1024,512]{1,0:T(8,128)(2,1)} %param.15), channel_id=1, source_target_pairs={{0,1},{1,0},{2,3},{3,2},{4,5},{5,4},{6,7},{7,6},{8,9},{9,8},{10,11... | collective-permute-start | bytes 3145736 | tf_op jit(solution)/shard_map/ppermute | solution.py:207
  81.6 15.6 %collective-permute-start.24 = (bf16[512,256]{1,0:T(8,128)(2,1)S(1)}, bf16[512,256]{1,0:T(8,128)(2,1)S(1)}, u32[]{:S(2)}, u32[]{:S(2)}) collective-permute-start(bf16[512,256]{1,0:T(8,128)(2,1)S(1)} %collective-permute-done.23), channel_id=1, source_target_pairs={{0,16},{8,24},{16,0},{24,8},{1,17},{9,25},{17,1},{25,9},{2,18},{10... | collective-permute-start | bytes 786440 | tf_op jit(solution)/shard_map/ppermute | solution.py:201
  85.4 26.1 %collective-permute-start.28 = (bf16[1024,512]{1,0:T(8,128)(2,1)S(1)}, bf16[1024,512]{1,0:T(8,128)(2,1)S(1)}, u32[]{:S(2)}, u32[]{:S(2)}) collective-permute-start(bf16[1024,512]{1,0:T(8,128)(2,1)S(1)} %copy-done.31), channel_id=1, source_target_pairs={{0,8},{8,0},{16,24},{24,16},{1,9},{9,1},{17,25},{25,17},{2,10},{10... | collective-permute-start | bytes 3145736 | tf_op jit(solution)/shard_map/ppermute | solution.py:197
  85.9 16.1 %collective-permute-start.26 = (bf16[512,256]{1,0:T(8,128)(2,1)S(1)}, bf16[512,256]{1,0:T(8,128)(2,1)S(1)}, u32[]{:S(2)}, u32[]{:S(2)}) collective-permute-start(bf16[512,256]{1,0:T(8,128)(2,1)S(1)} %collective-permute-done.25), channel_id=1, source_target_pairs={{0,16},{8,24},{16,0},{24,8},{1,17},{9,25},{17,1},{25,9},{2,18},{10... | collective-permute-start | bytes 786440 | tf_op jit(solution)/shard_map/ppermute | solution.py:201
  91.5 40.7 %collective-permute-start.31 = (bf16[1024,512]{1,0:T(8,128)(2,1)S(1)}, bf16[1024,512]{1,0:T(8,128)(2,1)S(1)}, u32[]{:S(2)}, u32[]{:S(2)}) collective-permute-start(bf16[1024,512]{1,0:T(8,128)(2,1)S(1)} %copy-done.29), channel_id=1, source_target_pairs={{0,8},{8,0},{16,24},{24,16},{1,9},{9,1},{17,25},{25,17},{2,10},{10... | collective-permute-start | bytes 3145736 | tf_op jit(solution)/shard_map/ppermute | solution.py:197
  97.1 35.1 %collective-permute-start.8 = (bf16[1024,512]{1,0:T(8,128)(2,1)S(1)}, bf16[1024,512]{1,0:T(8,128)(2,1)S(1)}, u32[]{:S(2)}, u32[]{:S(2)}) collective-permute-start(bf16[1024,512]{1,0:T(8,128)(2,1)S(1)} %copy-done.29), channel_id=1, source_target_pairs={{0,1},{1,0},{2,3},{3,2},{4,5},{5,4},{6,7},{7,6},{8,9},{9,8},{10,11... | collective-permute-start | bytes 3145736 | tf_op jit(solution)/shard_map/ppermute | solution.py:207
  111.5 26.1 %collective-permute-start.29 = (bf16[1024,512]{1,0:T(8,128)(2,1)S(1)}, bf16[1024,512]{1,0:T(8,128)(2,1)S(1)}, u32[]{:S(2)}, u32[]{:S(2)}) collective-permute-start(bf16[1024,512]{1,0:T(8,128)(2,1)S(1)} %collective-permute-done.28), channel_id=1, source_target_pairs={{0,1},{1,0},{2,3},{3,2},{4,5},{5,4},{6,7},{7,6},{8,9},{9,8},{10,11... | collective-permute-start | bytes 3145736 | tf_op jit(solution)/shard_map/ppermute | solution.py:207
  265.3 43.8 %collective-permute-start.38 = (f32[4,512]{1,0:T(4,128)S(1)}, f32[4,512]{1,0:T(4,128)S(1)}, u32[]{:S(2)}, u32[]{:S(2)}) collective-permute-start(f32[4,512]{1,0:T(4,128)S(1)} %constant_dynamic-slice_fusion), channel_id=1, source_target_pairs={{0,1},{1,0},{2,3},{3,2},{4,5},{5,4},{6,7},{7,6},{8,9},{9,8},{10,11... | collective-permute-start | bytes 24584 | tf_op jit(solution)/shard_map/ppermute | solution.py:207
  270.7 80.2 %collective-permute-start.39 = (bf16[1024,3,128]{0,2,1:T(8,128)(2,1)S(1)}, bf16[1024,3,128]{0,2,1:T(8,128)(2,1)S(1)}, u32[]{:S(2)}, u32[]{:S(2)}) collective-permute-start(bf16[1024,3,128]{0,2,1:T(8,128)(2,1)S(1)} %slice.267), channel_id=1, source_target_pairs={{0,16},{8,24},{16,0},{24,8},{1,17},{9,25},{17,1},{25,9},{2,18},{10... | collective-permute-start | bytes 2359304 | tf_op jit(solution)/shard_map/ppermute | solution.py:201
  272.5 23.8 %collective-permute-start.45 = (bf16[128,1024]{1,0:T(8,128)(2,1)S(1)}, bf16[128,1024]{1,0:T(8,128)(2,1)S(1)}, u32[]{:S(2)}, u32[]{:S(2)}) collective-permute-start(bf16[128,1024]{1,0:T(8,128)(2,1)S(1)} %slice.270), channel_id=1, source_target_pairs={{0,16},{8,24},{16,0},{24,8},{1,17},{9,25},{17,1},{25,9},{2,18},{10... | collective-permute-start | bytes 786440 | tf_op jit(solution)/shard_map/ppermute | solution.py:201
  303.2 67.2 %collective-permute-start.51 = (bf16[1024,512]{0,1:T(8,128)(2,1)S(1)}, bf16[1024,512]{0,1:T(8,128)(2,1)S(1)}, u32[]{:S(2)}, u32[]{:S(2)}) collective-permute-start(bf16[1024,512]{0,1:T(8,128)(2,1)S(1)} %slice.266), channel_id=1, source_target_pairs={{0,16},{8,24},{16,0},{24,8},{1,17},{9,25},{17,1},{25,9},{2,18},{10... | collective-permute-start | bytes 3145736 | tf_op jit(solution)/shard_map/ppermute | solution.py:201
  307.0 63.9 %collective-permute-start.57 = (bf16[512,1024]{1,0:T(8,128)(2,1)S(1)}, bf16[512,1024]{1,0:T(8,128)(2,1)S(1)}, u32[]{:S(2)}, u32[]{:S(2)}) collective-permute-start(bf16[512,1024]{1,0:T(8,128)(2,1)S(1)} %slice.265), channel_id=1, source_target_pairs={{0,16},{8,24},{16,0},{24,8},{1,17},{9,25},{17,1},{25,9},{2,18},{10... | collective-permute-start | bytes 3145736 | tf_op jit(solution)/shard_map/ppermute | solution.py:201
  307.6 42.7 %collective-permute-start.49 = (bf16[128,256]{1,0:T(8,128)(2,1)S(1)}, bf16[128,256]{1,0:T(8,128)(2,1)S(1)}, u32[]{:S(2)}, u32[]{:S(2)}) collective-permute-start(bf16[128,256]{1,0:T(8,128)(2,1)S(1)} %add_convert_fusion.7), channel_id=1, source_target_pairs={{0,16},{8,24},{16,0},{24,8},{1,17},{9,25},{17,1},{25,9},{2,18},{10... | collective-permute-start | bytes 196616 | tf_op jit(solution)/shard_map/ppermute | solution.py:201
  370.9 37.2 %collective-permute-start.53 = (bf16[256,512]{0,1:T(8,128)(2,1)S(1)}, bf16[256,512]{0,1:T(8,128)(2,1)S(1)}, u32[]{:S(2)}, u32[]{:S(2)}) collective-permute-start(bf16[256,512]{0,1:T(8,128)(2,1)S(1)} %get-tuple-element.111), channel_id=1, source_target_pairs={{0,4},{2,6},{4,0},{6,2},{1,5},{3,7},{5,1},{7,3},{8,12},{10,14},{12... | collective-permute-start | bytes 786440 | tf_op jit(solution)/shard_map/ppermute | solution.py:204
  373.3 34.8 %collective-permute-start.52 = (bf16[256,512]{0,1:T(8,128)(2,1)S(1)}, bf16[256,512]{0,1:T(8,128)(2,1)S(1)}, u32[]{:S(2)}, u32[]{:S(2)}) collective-permute-start(bf16[256,512]{0,1:T(8,128)(2,1)S(1)} %get-tuple-element.109), channel_id=1, source_target_pairs={{0,2},{2,4},{4,6},{6,0},{1,3},{3,5},{5,7},{7,1},{8,10},{10,12},{12... | collective-permute-start | bytes 786440 | tf_op jit(solution)/shard_map/ppermute | solution.py:204
  376.9 32.9 %collective-permute-start.60 = (bf16[512,256]{1,0:T(8,128)(2,1)S(1)}, bf16[512,256]{1,0:T(8,128)(2,1)S(1)}, u32[]{:S(2)}, u32[]{:S(2)}) collective-permute-start(bf16[512,256]{1,0:T(8,128)(2,1)S(1)} %get-tuple-element.107), channel_id=1, source_target_pairs={{0,6},{2,0},{4,2},{6,4},{1,7},{3,1},{5,3},{7,5},{8,14},{10,8},{12,... | collective-permute-start | bytes 786440 | tf_op jit(solution)/shard_map/ppermute | solution.py:204
  380.2 37.2 %collective-permute-start.59 = (bf16[512,256]{1,0:T(8,128)(2,1)S(1)}, bf16[512,256]{1,0:T(8,128)(2,1)S(1)}, u32[]{:S(2)}, u32[]{:S(2)}) collective-permute-start(bf16[512,256]{1,0:T(8,128)(2,1)S(1)} %get-tuple-element.108), channel_id=1, source_target_pairs={{0,4},{2,6},{4,0},{6,2},{1,5},{3,7},{5,1},{7,3},{8,12},{10,14},{12... | collective-permute-start | bytes 786440 | tf_op jit(solution)/shard_map/ppermute | solution.py:204
  381.6 37.3 %collective-permute-start.58 = (bf16[512,256]{1,0:T(8,128)(2,1)S(1)}, bf16[512,256]{1,0:T(8,128)(2,1)S(1)}, u32[]{:S(2)}, u32[]{:S(2)}) collective-permute-start(bf16[512,256]{1,0:T(8,128)(2,1)S(1)} %get-tuple-element.106), channel_id=1, source_target_pairs={{0,2},{2,4},{4,6},{6,0},{1,3},{3,5},{5,7},{7,1},{8,10},{10,12},{12... | collective-permute-start | bytes 786440 | tf_op jit(solution)/shard_map/ppermute | solution.py:204
  408.1 150.3 %collective-permute-start.27 = (bf16[1024,512]{1,0:T(8,128)(2,1)}, bf16[1024,512]{1,0:T(8,128)(2,1)}, u32[]{:S(2)}, u32[]{:S(2)}) collective-permute-start(bf16[1024,512]{1,0:T(8,128)(2,1)} %constant_dynamic-slice_fusion.5), channel_id=1, source_target_pairs={{0,1},{1,0},{2,3},{3,2},{4,5},{5,4},{6,7},{7,6},{8,9},{9,8},{10,11... | collective-permute-start | bytes 3145736 | tf_op jit(solution)/shard_map/ppermute | solution.py:207
  409.8 26.9 %collective-permute-start.35 = (bf16[1024,512]{1,0:T(8,128)(2,1)}, bf16[1024,512]{1,0:T(8,128)(2,1)}, u32[]{:S(2)}, u32[]{:S(2)}) collective-permute-start(bf16[1024,512]{1,0:T(8,128)(2,1)} %constant_dynamic-slice_fusion.3), channel_id=1, source_target_pairs={{0,1},{1,0},{2,3},{3,2},{4,5},{5,4},{6,7},{7,6},{8,9},{9,8},{10,11... | collective-permute-start | bytes 3145736 | tf_op jit(solution)/shard_map/ppermute | solution.py:207
  417.4 141.0 %collective-permute-start.34 = (bf16[1024,512]{1,0:T(8,128)(2,1)}, bf16[1024,512]{1,0:T(8,128)(2,1)}, u32[]{:S(2)}, u32[]{:S(2)}) collective-permute-start(bf16[1024,512]{1,0:T(8,128)(2,1)} %add_convert_fusion.3), channel_id=1, source_target_pairs={{0,8},{8,0},{16,24},{24,16},{1,9},{9,1},{17,25},{25,17},{2,10},{10... | collective-permute-start | bytes 3145736 | tf_op jit(solution)/shard_map/ppermute | solution.py:197
  419.0 47.3 %collective-permute-start.37 = (bf16[1024,512]{1,0:T(8,128)(2,1)}, bf16[1024,512]{1,0:T(8,128)(2,1)}, u32[]{:S(2)}, u32[]{:S(2)}) collective-permute-start(bf16[1024,512]{1,0:T(8,128)(2,1)} %add_convert_fusion.2), channel_id=1, source_target_pairs={{0,8},{8,0},{16,24},{24,16},{1,9},{9,1},{17,25},{25,17},{2,10},{10... | collective-permute-start | bytes 3145736 | tf_op jit(solution)/shard_map/ppermute | solution.py:197
  434.3 43.1 %collective-permute-start.56 = (bf16[256,1024]{0,1:T(8,128)(2,1)S(1)}, bf16[256,1024]{0,1:T(8,128)(2,1)S(1)}, u32[]{:S(2)}, u32[]{:S(2)}) collective-permute-start(bf16[256,1024]{0,1:T(8,128)(2,1)S(1)} %pad_maximum_fusion.6), channel_id=1, source_target_pairs={{0,8},{8,0},{16,24},{24,16},{1,9},{9,1},{17,25},{25,17},{2,10},{10... | collective-permute-start | bytes 1572872 | tf_op jit(solution)/shard_map/ppermute | solution.py:197
  436.7 118.9 %collective-permute-start.62 = (bf16[1024,256]{1,0:T(8,128)(2,1)}, bf16[1024,256]{1,0:T(8,128)(2,1)}, u32[]{:S(2)}, u32[]{:S(2)}) collective-permute-start(bf16[1024,256]{1,0:T(8,128)(2,1)} %pad_maximum_fusion.7), channel_id=1, source_target_pairs={{0,8},{8,0},{16,24},{24,16},{1,9},{9,1},{17,25},{25,17},{2,10},{10... | collective-permute-start | bytes 1572872 | tf_op jit(solution)/shard_map/ppermute | solution.py:197
  (116 other events, 1315.2 us)

commit v2 on v1

--- a/solution.py
+++ b/solution.py
@@ -183,6 +183,328 @@
     )(normed, cot, up_weight, up_bias, down_weight)
 
 
+MESH = pl.DeviceIdType.MESH
+
+
+class Net:
+    def __init__(self, send_sems, recv_sems):
+        self.send_sems, self.recv_sems = send_sems, recv_sems
+        self.slots = {}
+        self.pending = []
+
+    def slot(self, key):
+        return self.slots.setdefault(key, len(self.slots))
+
+    def make(self, key, source, target, device):
+        i = self.slot(key)
+        return pltpu.make_async_remote_copy(
+            src_ref=source,
+            dst_ref=target,
+            send_sem=self.send_sems.at[i],
+            recv_sem=self.recv_sems.at[i],
+            device_id=device,
+            device_id_type=MESH,
+        )
+
+    def send(self, key, source, target, device):
+        copy = self.make(key, source, target, device)
+        copy.start()
+        self.pending.append(copy)
+
+    def wait(self, key, landed, device):
+        self.make(key, landed, landed, device).wait_recv()
+
+    def drain(self):
+        for copy in self.pending:
+            copy.wait_send()
+        self.pending = []
+
+
+def spread(columns, width):
+    return jnp.concatenate([columns] * (width // LANES), axis=1)
+
+
+def attend_pair(mix, base, gc, gc_base, ctx, seg_row, seg_col, cos_tab, sin_tab, dk_acc, dv_acc, block):
+    length = mix.shape[0]
+    lane = lax.broadcasted_iota(jnp.int32, (1, LANES), 1)
+    low_lanes = lane % HEAD_DIM < ROT // 2
+    first = lane < HEAD_DIM
+    zero = jnp.zeros((), BF16)
+    cols = [pl.ds(base + i * LANES, LANES) for i in range(3)]
+    head_cols = pl.ds(gc_base, LANES)
+
+    def split(values):
+        return [jnp.where(first, values, zero), jnp.where(first, zero, values)]
+
+    dk_acc[...] = jnp.zeros_like(dk_acc)
+    dv_acc[...] = jnp.zeros_like(dv_acc)
+    for begin in range(0, length, block):
+        low = max(0, begin - (MAX_DOC - 1)) // LANES * LANES
+        width = begin + block - low
+        rows = pl.ds(begin, block)
+        keys = pl.ds(low, width)
+        q_parts = split(mix[rows, cols[0]] * jnp.asarray(HEAD_DIM**-0.5, BF16))
+        g_parts = split(gc[rows, head_cols])
+        k_block = mix[keys, cols[1]]
+        v_block = mix[keys, cols[2]]
+        places = begin + lax.broadcasted_iota(jnp.int32, (block, width), 0)
+        key_places = low + lax.broadcasted_iota(jnp.int32, (block, width), 1)
+        allowed = (spread(seg_col[rows, :], width) == seg_row[0:1, keys]) & (places >= key_places)
+        probs = []
+        grads = []
+        for part in range(2):
+            scores = dot(q_parts[part], k_block, NT)
+            scores = jnp.where(allowed, scores, -1e30)
+            top = jnp.max(scores, axis=1, keepdims=True)
+            powers = jnp.exp(scores - top)
+            total = jnp.sum(powers, axis=1, keepdims=True)
+            chances = powers * (1.0 / total)
+            slopes = dot(g_parts[part], v_block, NT)
+            inner = jnp.sum(slopes * chances, axis=1, keepdims=True)
+            probs.append(chances.astype(BF16))
+            grads.append((chances * (slopes - inner)).astype(BF16))
+        ctx[rows, head_cols] = jnp.where(first, dot(probs[0], v_block), dot(probs[1], v_block)).astype(BF16)
+        dq = jnp.where(first, dot(grads[0], k_block), dot(grads[1], k_block)) * HEAD_DIM**-0.5
+        mix[rows, cols[0]] = turn(dq, cos_tab[rows, :], -sin_tab[rows, :], low_lanes).astype(BF16)
+        dk_acc[keys, :] += dot(grads[0], q_parts[0], TN) + dot(grads[1], q_parts[1], TN)
+        dv_acc[keys, :] += dot(probs[0], g_parts[0], TN) + dot(probs[1], g_parts[1], TN)
+    mix[:, cols[1]] = turn(dk_acc[...], cos_tab[...], -sin_tab[...], low_lanes).astype(BF16)
+    mix[:, cols[2]] = dv_acc[...].astype(BF16)
+
+
+def first_kernel(
+    hidden, cot, wq_in, wo_in, wu_in, wd_in, rows_in, params_in, bq_in, freq_in,
+    x_out, g_out, a_out, wq_out, wo_out, wu_out, wd_out, mix_out, ctx_out, rows_out, params_out,
+    X, G, A, WQ, WO, WU, WD, MIX, GC, CTX, rows_far, params, seg_col, cos_tab, sin_tab, dk_acc, dv_acc,
+    send_sems, recv_sems, local_sems, *, rows_n,
+):
+    R = rows_n
+    dp, row, col = lax.axis_index("dp"), lax.axis_index("row"), lax.axis_index("col")
+    side, quarter = lax.rem(dp, 2), lax.div(dp, 2)
+    length, half = hidden.shape
+    shard = wq_in.shape[0]
+    core = (dp, row, 1 - col)
+    xdev = (dp + 1 - 2 * side, row, col)
+    ydev = (side + 2 * (1 - quarter), row, col)
+
+    def zdev(t):
+        return (dp, lax.rem(row + t + R, R), col)
+
+    barrier = pltpu.get_barrier_semaphore()
+    peers = [core, xdev, ydev] + [zdev(t) for t in range(1, R)]
+    for peer in peers:
+        pl.semaphore_signal(barrier, inc=1, device_id=peer, device_id_type=MESH)
+    pl.semaphore_wait(barrier, len(peers))
+
+    net = Net(send_sems, recv_sems)
+    own_cols = pl.ds(pl.multiple_of(col * half, half), half)
+    far_cols = pl.ds(pl.multiple_of((1 - col) * half, half), half)
+    local = []
+
+    def move(source, target):
+        copy = pltpu.make_async_copy(source, target, local_sems.at[len(local)])
+        copy.start()
+        local.append(copy)
+        return copy
+
+    net.send("core h", hidden, X.at[0, :, own_cols], core)
+    net.send("core p", params_in, params.at[:, own_cols], core)
+    net.send("x rows", rows_in, rows_far, xdev)
+    here_h = move(hidden, X.at[0, :, own_cols])
+    here_p = move(params_in, params.at[:, own_cols])
+
+    qc = WQ.shape[1] // 2
+    oc = WO.shape[0] // 2
+    uc = WU.shape[1] // 2
+    unit_at = pl.multiple_of((side * 2 + quarter) * uc, uc)
+    unit_other = pl.multiple_of((side * 2 + 1 - quarter) * uc, uc)
+    head_at = pl.multiple_of((side * 2 + quarter) * oc, oc)
+    head_other = pl.multiple_of((side * 2 + 1 - quarter) * oc, oc)
+
+    def block(t):
+        return pl.ds(pl.multiple_of(lax.rem(row + t + R, R) * shard, shard), shard)
+
+    weights = {
+        "q": (wq_in.at[:, pl.ds(0, qc)], wq_in.at[:, pl.ds(qc, qc)], lambda t, h: WQ.at[block(t), pl.ds(h * qc, qc)]),
+        "o": (wo_in.at[pl.ds(head_at, oc), :], wo_in.at[pl.ds(head_other, oc), :], lambda t, h: WO.at[pl.ds(h * oc, oc), block(t)]),
+        "u": (wu_in.at[:, pl.ds(unit_at, uc)], wu_in.at[:, pl.ds(unit_other, uc)], lambda t, h: WU.at[block(t), pl.ds(h * uc, uc)]),
+        "d": (wd_in.at[pl.ds(unit_at, uc), :], wd_in.at[pl.ds(unit_other, uc), :], lambda t, h: WD.at[pl.ds(h * uc, uc), block(t)]),
+    }
+    here_w = {}
+    for name, (mine, other, place) in weights.items():
+        net.send((name, 1), mine, place(0, 0), zdev(-1))
+        if R > 2:
+            net.send((name, R - 1), mine, place(0, 0), zdev(1))
+        if name == "q":
+            here_w[name] = [move(mine, place(0, 0)), move(other, place(0, 1))]
+    chunks = 2
+    piece = length // chunks
+    for c in range(chunks):
+        span = pl.ds(c * piece, piece)
+        net.send(("x h", c), hidden.at[span, :], X.at[1, span, own_cols], xdev)
+    net.send("core g", cot, G.at[0, :, own_cols], core)
+    here_g = move(cot, G.at[0, :, own_cols])
+    for c in range(chunks):
+        span = pl.ds(c * piece, piece)
+        net.send(("x g", c), cot.at[span, :], G.at[1, span, own_cols], xdev)
+    for name in "oud":
+        mine, other, place = weights[name]
+        here_w[name] = [move(mine, place(0, 0)), move(other, place(0, 1))]
+
+    def along(name, t):
+        place = weights[name][2]
+        net.wait((name, t), place(t, 0), zdev(t))
+        if t < R // 2:
+            net.send((name, t + 1), place(t, 0), place(t, 0), zdev(-1))
+        elif R // 2 + 1 < t:
+            net.send((name, t - 1), place(t, 0), place(t, 0), zdev(1))
+        net.send((name, t, "y"), place(t, 0), place(t, 1), ydev)
+
+    order = [1, R - 1] + [t for t in range(2, R - 1)] if R > 2 else [1]
+
+    def arrive(name):
+        place = weights[name][2]
+        for copy in here_w[name]:
+            copy.wait()
+        for t in range(1, R):
+            net.wait((name, t, "y"), place(t, 1), ydev)
+
+    def hand_over(name, buffer, c):
+        span = pl.ds(c * piece, piece)
+        net.wait(("x " + name, c), buffer.at[1, span, own_cols], xdev)
+        net.send(("core far " + name, c), buffer.at[1, span, own_cols], buffer.at[1, span, own_cols], core)
+
+    tile = 256
+    gain_one, shift_one = 0, 1
+
+    def norm(s, at, gain, shift):
+        values = X[s, at, :].astype(F32)
+        centred = values - jnp.mean(values, axis=-1, keepdims=True)
+        inv = lax.rsqrt(jnp.mean(centred * centred, axis=-1, keepdims=True) + EPS)
+        A[s, at, :] = (centred * inv * params[gain : gain + 1, :] + params[shift : shift + 1, :]).astype(BF16)
+
+    def each_tile(body):
+        @pl.loop(0, length // tile)
+        def _(i):
+            body(pl.ds(pl.multiple_of(i * tile, tile), tile))
+
+    lane = lax.broadcasted_iota(jnp.int32, (1, LANES), 1)
+    low_lanes = lane % HEAD_DIM < ROT // 2
+
+    def tables(rows):
+        columns = jnp.transpose(jnp.broadcast_to(rows[0:1, :], (LANES, length)))
+        seg_col[...] = columns
+        columns = jnp.transpose(jnp.broadcast_to(rows[1:2, :], (LANES, length)))
+        angles = columns * freq_in[0:1, :]
+        cos_tab[...] = jnp.cos(angles)
+        sin_tab[...] = jnp.sin(angles) * freq_in[1:2, :]
+
+    def project(s):
+        def body(at):
+            mixed = dot(A[s, at, :], WQ[...]) + bq_in[...]
+            for i in range(mixed.shape[1] // LANES):
+                part = mixed[:, i * LANES : (i + 1) * LANES]
+                if i % 3 < 2:
+                    part = turn(part, cos_tab[at, :], sin_tab[at, :], low_lanes)
+                MIX[s, at, pl.ds(i * LANES, LANES)] = part.astype(BF16)
+
+        each_tile(body)
+
+    def pull_context(s):
+        def body(at):
+            GC[at, :] = dot(G[s, at, :], WO[...], NT).astype(BF16)
+
+        each_tile(body)
+
+    def attend(s, rows, pair):
+        attend_pair(
+            MIX.at[s], pair * 3 * LANES, GC, pair * LANES, CTX.at[s], rows, seg_col, cos_tab, sin_tab, dk_acc, dv_acc, tile
+        )
+
+    pairs = CTX.shape[2] // LANES
+    tables(rows_in)
+    here_h.wait()
+    here_p.wait()
+    net.wait("core h", X.at[0, :, far_cols], core)
+    net.wait("core p", params.at[:, far_cols], core)
+    each_tile(lambda at: norm(0, at, gain_one, shift_one))
+    for t in order:
+        along("q", t)
+    for t in order:
+        along("o", t)
+    arrive("q")
+    project(0)
+    here_g.wait()
+    net.wait("core g", G.at[0, :, far_cols], core)
+    hand_over("h", X, 0)
+    arrive("o")
+    pull_context(0)
+    along("u", 1)
+    along("u", R - 1)
+    for pair in range(pairs):
+        attend(0, rows_in, pair)
+        hand_over("h" if pair == 0 else "g", X if pair == 0 else G, 1 if pair == 0 else 0)
+        along("d", 1 if pair == 0 else R - 1)
+        for t in order[2:]:
+            along("u" if pair == 0 else "d", t)
+    for c in range(chunks):
+        span = pl.ds(c * piece, piece)
+        net.wait(("core far h", c), X.at[1, span, far_cols], core)
+    net.wait("x rows", rows_far, xdev)
+    tables(rows_far)
+    each_tile(lambda at: norm(1, at, gain_one, shift_one))
+    project(1)
+    hand_over("g", G, 1)
+    for c in range(chunks):
+        span = pl.ds(c * piece, piece)
+        net.wait(("core far g", c), G.at[1, span, far_cols], core)
+    pull_context(1)
+    for pair in range(pairs):
+        attend(1, rows_far, pair)
+    arrive("u")
+    arrive("d")
+    net.drain()
+    done = [
+        move(a, b)
+        for a, b in [
+            (X, x_out), (G, g_out), (A, a_out), (WQ, wq_out), (WO, wo_out), (WU, wu_out), (WD, wd_out),
+            (MIX, mix_out), (CTX, ctx_out), (rows_far, rows_out), (params, params_out),
+        ]
+    ]
+    for copy in done:
+        copy.wait()
+
+
+def first(hidden, cot, wq, wo, wu, wd, rows, params, bq, freq, rows_n):
+    length, half = hidden.shape
+    width = 2 * half
+    wide3 = wq.shape[1]
+    wide = wide3 // 3
+    units = wu.shape[1] // 2
+    arrays = [
+        ((2, length, width), BF16), ((2, length, width), BF16), ((2, length, width), BF16),
+        ((width, wide3), BF16), ((wide, width), BF16), ((width, units), BF16), ((units, width), BF16),
+        ((2, length, wide3), BF16), ((2, length, wide), BF16), (rows.shape, F32), ((params.shape[0], width), F32),
+    ]
+    out_shape = [jax.ShapeDtypeStruct(shape, kind) for shape, kind in arrays]
+    buffers = [pltpu.VMEM(shape, kind) for shape, kind in arrays]
+    buffers.insert(8, pltpu.VMEM((length, wide), BF16))
+    table = pltpu.VMEM((length, LANES), F32)
+    any_spec = pl.BlockSpec(memory_space=pl.ANY)
+    vmem_spec = pl.BlockSpec(memory_space=pltpu.VMEM)
+    return pl.pallas_call(
+        functools.partial(first_kernel, rows_n=rows_n),
+        out_shape=out_shape,
+        in_specs=[any_spec] * 6 + [vmem_spec] * 4,
+        out_specs=[any_spec] * len(out_shape),
+        scratch_shapes=buffers + [table] * 5 + [
+            pltpu.SemaphoreType.DMA((80,)), pltpu.SemaphoreType.DMA((80,)), pltpu.SemaphoreType.DMA((32,)),
+        ],
+        compiler_params=pltpu.CompilerParams(collective_id=0, has_side_effects=True, vmem_limit_bytes=60 << 20),
+        name="first",
+    )(hidden, cot, wq, wo, wu, wd, rows, params, bq, freq)
+
+
 def normalize(values):
     centred = values - jnp.mean(values, axis=-1, keepdims=True)
     variance = jnp.mean(centred * centred, axis=-1, keepdims=True)
@@ -190,7 +512,7 @@
     return centred * inv_std, inv_std
 
 
-def make_local(groups, rows, cols):
+def make_general(groups, rows, cols):
     quarters = groups // 2
 
     def pair_swap(value):
@@ -456,6 +778,258 @@
     return local
 
 
+def make_fast(groups, rows, cols):
+    quarters = groups // 2
+
+    def pair_swap(value):
+        return lax.ppermute(value, "dp", [(d, d ^ 1) for d in range(groups)])
+
+    def quarter_shift(value, shift):
+        moves = [(2 * a + b, 2 * ((a + shift) % quarters) + b) for a in range(quarters) for b in range(2)]
+        return lax.ppermute(value, "dp", moves)
+
+    def row_shift(value, shift):
+        return lax.ppermute(value, "row", [(r, (r + shift) % rows) for r in range(rows)])
+
+    def core_swap(value):
+        return lax.ppermute(value, "col", [(0, 1), (1, 0)])
+
+    def local(
+        hidden,
+        segments,
+        ln1_gain,
+        ln1_bias,
+        qkv_weight,
+        qkv_bias,
+        out_weight,
+        out_bias,
+        ln2_gain,
+        ln2_bias,
+        up_weight,
+        up_bias,
+        down_weight,
+        down_bias,
+        cotangent,
+    ):
+        assert segments.shape[0] == 1 and cols == 2
+        length = segments.shape[1]
+        half_width = hidden.shape[1]
+        width = 2 * half_width
+        shard = qkv_weight.shape[0]
+        heads = qkv_weight.shape[1] // (3 * HEAD_DIM) // 2
+        wide = heads * HEAD_DIM
+        units = up_weight.shape[1] // 2
+        whole_heads = heads % quarters == 0
+        dp = lax.axis_index("dp")
+        row = lax.axis_index("row")
+        col = lax.axis_index("col")
+        side = lax.rem(dp, 2)
+        quarter = dp // 2
+
+        def both(mine, other):
+            flip = col == 0
+            return jnp.concatenate([jnp.where(flip, mine, other), jnp.where(flip, other, mine)], axis=-1)
+
+        def half_of(value, axis):
+            size = value.shape[axis] // 2
+            return lax.dynamic_slice_in_dim(value, side * size, size, axis)
+
+        def piece_of(value, shift, axis, placed=False):
+            size = value.shape[axis] // quarters
+            if placed:
+                return lax.slice_in_dim(value, shift * size, (shift + 1) * size, axis=axis)
+            return lax.dynamic_slice_in_dim(value, lax.rem(quarter - shift + quarters, quarters) * size, size, axis)
+
+        def in_place(pieces, axis):
+            if quarters == 1:
+                return pieces[0]
+            if quarters == 2:
+                flip = quarter == 0
+                first = jnp.where(flip, pieces[0], pieces[1])
+                second = jnp.where(flip, pieces[1], pieces[0])
+                return jnp.concatenate([first, second], axis=axis)
+            order = lax.rem(quarter - jnp.arange(quarters) + quarters, quarters)
+            stacked = jnp.take(jnp.stack(pieces), order, axis=0)
+            return jnp.concatenate([stacked[i] for i in range(quarters)], axis=axis)
+
+        def near(pieces, axis, keep):
+            return jnp.concatenate(pieces, axis=axis) if keep else in_place(pieces, axis)
+
+        def gather(value, width_axis, unit_axis, keep):
+            mine = piece_of(value, 0, unit_axis)
+            received = {0: mine}
+            ahead = behind = mine
+            for step in range(1, rows):
+                if step <= rows // 2:
+                    ahead = row_shift(ahead, -1)
+                    received[step] = ahead
+                if step <= (rows - 1) // 2:
+                    behind = row_shift(behind, 1)
+                    received[rows - step] = behind
+            result = jnp.zeros(
+                [width if i == width_axis else n for i, n in enumerate(value.shape)], value.dtype
+            )
+            for step in range(rows):
+                if step == 0:
+                    pieces = [piece_of(value, q, unit_axis) for q in range(quarters)]
+                else:
+                    pieces = [received[step]]
+                    pieces += [quarter_shift(received[step], q) for q in range(1, quarters)]
+                block = near(pieces, unit_axis, keep)
+                place = lax.rem(row + step, rows) * shard
+                result = lax.dynamic_update_slice_in_dim(result, block, place, width_axis)
+            return result
+
+        place = jnp.arange(length, dtype=jnp.int32)
+        before = segments[0][None, :] < segments[0][:, None]
+        position = place - jnp.sum(before.astype(jnp.int32), axis=1)
+        rows_own = jnp.stack([segments[0].astype(F32), position.astype(F32)] + [jnp.zeros((length,), F32)] * 6)
+        params = jnp.stack([ln1_gain, ln1_bias, ln2_gain, ln2_bias] * 2).astype(F32)
+        lane = jnp.arange(LANES) % HEAD_DIM
+        frequency = 10000.0 ** (-2.0 * (lane % (ROT // 2)).astype(F32) / ROT)
+        sign = jnp.where(lane < ROT // 2, -1.0, 1.0)
+        turning = lane < ROT
+        freq = jnp.stack([jnp.where(turning, frequency, 0.0), jnp.where(turning, sign, 0.0)] * 4).astype(F32)
+
+        def by_quarter(value):
+            n = value.shape[0]
+            value = value.reshape(n, 2, quarters, heads // quarters, 3, HEAD_DIM)
+            value = lax.dynamic_index_in_dim(value, side, 1, keepdims=False)
+            value = jnp.swapaxes(value, 2, 3).reshape(n, quarters, 3 * wide // quarters)
+            flip = quarter == 0
+            mine = jnp.where(flip, value[:, 0], value[:, 1])
+            other = jnp.where(flip, value[:, 1], value[:, 0])
+            return jnp.concatenate([mine, other], axis=1)
+
+        wq = by_quarter(qkv_weight)
+        bq = by_quarter(qkv_bias[None, :]).astype(F32)
+        up_half = half_of(up_bias, 0)
+        up_row = jnp.concatenate([piece_of(up_half, q, 0) for q in range(quarters)])[None, :].astype(F32)
+        x_all, g_all, a_all, qkv_all, out_all, up_all, down_all, mixes, ctxs, rows_far, params = first(
+            hidden, cotangent, wq, out_weight, up_weight, down_weight, rows_own, params, bq, freq, rows
+        )
+        gain_one, shift_one, gain_two, shift_two = [params[i][None, :] for i in range(4)]
+        cots = [g_all[0], g_all[1]]
+        norms = []
+        for index in range(2):
+            unit, inv = normalize(x_all[index].astype(F32))
+            norms.append((unit, inv, a_all[index], (unit * gain_two + shift_two).astype(BF16)))
+        contexts = [ctxs[0], ctxs[1]]
+        grads_mixed = [mixes[0], mixes[1]]
+
+        feeds = [feed(norm[3], cot, up_all, up_row, down_all) for norm, cot in zip(norms, cots)]
+
+        def reduce_grad(left, right, width_axis, unit_axis, placed, shape=None):
+            total = dot(left[0], right[0], TN) + dot(left[1], right[1], TN)
+            if shape is not None:
+                total = total.reshape(shape)
+            mine = piece_of(total, 0, unit_axis, placed)
+            for q in range(1, quarters):
+                part = piece_of(total, q, unit_axis, placed).astype(BF16)
+                mine = mine + quarter_shift(part, -q).astype(F32)
+            cut = lambda t: lax.dynamic_slice_in_dim(mine, lax.rem(row + t, rows) * shard, shard, width_axis)
+            result = cut(0)
+            for t in range(1, rows):
+                result = result + row_shift(cut(t).astype(BF16), t).astype(F32)
+            result = result.astype(BF16)
+            pieces = [result] + [quarter_shift(result, q) for q in range(1, quarters)]
+            result = in_place(pieces, unit_axis)
+            far = pair_swap(result)
+            flip = side == 0
+            return jnp.concatenate(
+                [jnp.where(flip, result, far), jnp.where(flip, far, result)], axis=unit_axis
+            ).astype(F32)
+
+        acts_one = [n[2] for n in norms]
+        acts_two = [n[3] for n in norms]
+        out_grad = reduce_grad(contexts, cots, 1, 0, whole_heads)
+        qkv_grad = reduce_grad(acts_one, grads_mixed, 0, 1, True)
+        down_grad = reduce_grad([f[0] for f in feeds], cots, 1, 0, True)
+        up_grad = reduce_grad(acts_two, [f[1] for f in feeds], 0, 1, True)
+        qkv_grad = qkv_grad.reshape(shard, 2 * quarters, 3, heads // quarters, HEAD_DIM)
+        qkv_grad = jnp.swapaxes(qkv_grad, 2, 3).reshape(shard, 6 * wide)
+
+        outs = []
+        slopes = []
+        norm_sums = jnp.zeros((4, width), F32)
+        for index in range(2):
+            unit, inv, _, _ = norms[index]
+            act, grad_up, _ = feeds[index]
+            outs.append((dot(contexts[index], out_all) + dot(act, down_all)).astype(BF16))
+            grad_one = dot(grads_mixed[index], qkv_all, NT)
+            grad_two = dot(grad_up, up_all, NT)
+            norm_sums += jnp.stack(
+                [
+                    jnp.sum(grad_one * unit, axis=0),
+                    jnp.sum(grad_one, axis=0),
+                    jnp.sum(grad_two * unit, axis=0),
+                    jnp.sum(grad_two, axis=0),
+                ]
+            )
+            scaled = grad_one * gain_one + grad_two * gain_two
+            mean_scaled = jnp.mean(scaled, axis=1, keepdims=True)
+            mean_unit = jnp.mean(scaled * unit, axis=1, keepdims=True)
+            slopes.append((inv * (scaled - mean_scaled - unit * mean_unit)).astype(BF16))
+
+        def fold(pair):
+            sums = []
+            for value in pair:
+                kept = lax.dynamic_slice_in_dim(value, col * half_width, half_width, 1).astype(F32)
+                given = lax.dynamic_slice_in_dim(value, (1 - col) * half_width, half_width, 1)
+                sums.append(kept + core_swap(given).astype(F32))
+            return sums[0] + pair_swap(sums[1].astype(BF16)).astype(F32)
+
+        cot_local = cotangent.astype(F32)
+        output = hidden.astype(F32) + fold(outs) + (out_bias.astype(F32) + down_bias.astype(F32))
+        input_grad = cot_local + fold(slopes)
+
+        qkv_sum = (
+            jnp.sum(grads_mixed[0].astype(F32), axis=0) + jnp.sum(grads_mixed[1].astype(F32), axis=0)
+        )
+        qkv_sum = in_place([piece_of(qkv_sum, q, 0, True) for q in range(quarters)], 0)
+        up_sum = (feeds[0][2] + feeds[1][2])[0]
+        up_sum = in_place([piece_of(up_sum, q, 0, True) for q in range(quarters)], 0)
+
+        def widen(value):
+            zeros = jnp.zeros_like(value)
+            flip = side == 0
+            return jnp.concatenate([jnp.where(flip, value, zeros), jnp.where(flip, zeros, value)], axis=-1)
+
+        kept = lax.dynamic_slice_in_dim(norm_sums, col * half_width, half_width, 1)
+        given = lax.dynamic_slice_in_dim(norm_sums, (1 - col) * half_width, half_width, 1)
+        norm_sums = kept + core_swap(given)
+        small = jnp.concatenate(
+            [widen(qkv_sum).reshape(-1), widen(up_sum), jnp.sum(cot_local, axis=0), norm_sums.reshape(-1)]
+        )
+        small = lax.psum(small, ("dp", "row"))
+        sizes = [6 * wide, 2 * units, half_width, half_width, half_width, half_width, half_width]
+        parts = []
+        start = 0
+        for size in sizes:
+            parts.append(lax.slice_in_dim(small, start, start + size))
+            start += size
+        qkv_sum, up_sum, cot_sum, gain_one_sum, shift_one_sum, gain_two_sum, shift_two_sum = parts
+        qkv_sum = jnp.swapaxes(qkv_sum.reshape(2 * quarters, 3, heads // quarters, HEAD_DIM), 1, 2).reshape(-1)
+        return (
+            output,
+            input_grad,
+            gain_one_sum,
+            shift_one_sum,
+            qkv_grad,
+            qkv_sum,
+            out_grad,
+            cot_sum,
+            gain_two_sum,
+            shift_two_sum,
+            up_grad,
+            up_sum,
+            down_grad,
+            cot_sum,
+        )
+
+    return local
+
+
 def solution(mesh):
     placed = (
         P(("dp", "row"), "col"),
@@ -474,8 +1048,10 @@
         P("col"),
         P(("dp", "row"), "col"),
     )
+    groups = mesh.shape["dp"]
+    make = make_fast if groups == 4 else make_general
     return jax.shard_map(
-        make_local(mesh.shape["dp"], mesh.shape["row"], mesh.shape["col"]),
+        make(mesh.shape["dp"], mesh.shape["row"], mesh.shape["col"]),
         mesh=mesh,
         in_specs=placed,
         out_specs=(

time: 571 us -> 481 us (0.84)
  waiting for transfers between devices: 192 us -> 110 us
  Pallas kernels: 42.3 us -> 117 us
  starting transfers between devices: 83.2 us -> 32 us
  other arithmetic: 61.6 us -> 45.2 us
  matrix products: 68.9 us -> 57.1 us
  local copies, waits for them, and re-layouts: 40.9 us -> 32.5 us
  blocking collectives: 72.2 us -> 79.6 us
    pallas_call x2 -> x1, Pallas kernels: 24.2 us -> 99.1 us  [first(): pl.pallas_call(functools.partial(first_kernel, rows_n=rows_n), out_shape=...]
    ppermute x20 -> x8, waiting for transfers between devices: 79.7 us -> 22 us  [quarter_shift(): return lax.ppermute(value, 'dp', moves)]
    ppermute x24 -> x12, starting transfers between devices: 53 us -> 16.1 us  [row_shift(): lax.ppermute(value, 'row', [(r, (r + shift) % rows) for r in range(rows)])]
    ppermute x9 -> x6, waiting for transfers between devices: 61.6 us -> 48 us  [pair_swap(): return lax.ppermute(value, 'dp', [(d, d ^ 1) for d in range(groups)])]
    dynamic_update_slice x16 -> x0, other arithmetic: 13 us -> none  [gather(): result = lax.dynamic_update_slice_in_dim(result, block, place, width_axis)]
    dot_general x20 -> x16, matrix products: 68.9 us -> 57.1 us  [dot(): return lax.dot_general(a, b, dims, preferred_element_type=F32)]
    ppermute x20 -> x8, starting transfers between devices: 20.4 us -> 8.99 us  [quarter_shift(): return lax.ppermute(value, 'dp', moves)]
    ppermute x24 -> x12, waiting for transfers between devices: 50.9 us -> 40.3 us  [row_shift(): lax.ppermute(value, 'row', [(r, (r + shift) % rows) for r in range(rows)])]
  transfers between devices with their start and end apart: 63 -> 31, of which waited for: 24 -> 15; matrix products, arithmetic and copies ran while one was open for 15% -> 19% of each run, Pallas kernels for 0% -> 0%
where the time goes in v2:
time: 481 us; the launch traced here: 476 us
  Pallas kernels  117 us (24%)
  waiting for transfers between devices  110 us (23%)
  blocking collectives  79.6 us (17%)
  matrix products  57.1 us (12%)
  other arithmetic  45.2 us (9%)
  local copies, waits for them, and re-layouts  32.5 us (7%)
  starting transfers between devices  32 us (7%)
    pallas_call x1, Pallas kernels, first(): pl.pallas_call(functools.partial(first_kernel, rows_n=rows_n), out_shape=...  99.1 us
    psum x1, blocking collectives, local(): small = lax.psum(small, ('dp', 'row'))  79.6 us
    dot_general x16, matrix products, dot(): return lax.dot_general(a, b, dims, preferred_element_type=F32)  57.1 us
    ppermute x6, waiting for transfers between devices, pair_swap(): return lax.ppermute(value, 'dp', [(d, d ^ 1) for d in range(groups)])  48 us
    ppermute x12, waiting for transfers between devices, row_shift(): lax.ppermute(value, 'row', [(r, (r + shift) % rows) for r in range(rows)])  40.3 us
    ppermute x8, waiting for transfers between devices, quarter_shift(): return lax.ppermute(value, 'dp', moves)  22 us
    pallas_call x2, Pallas kernels, feed(): pl.pallas_call(functools.partial(feed_kernel, chunk=min(256, units)), gri...  18.2 us
    ppermute x12, starting transfers between devices, row_shift(): lax.ppermute(value, 'row', [(r, (r + shift) % rows) for r in range(rows)])  16.1 us
  transfers between devices with their start and end apart: 31, of which 15 were waited for; matrix products, arithmetic and copies ran while one was open for 19% of the time, Pallas kernels for 0%

profile of v2, /device:TPU:0, one launch (start us, length us, event | category | flops | bytes accessed | tf_op | source)
XLA Modules:
  0.0 476.0 jit_solution(11284964681196036866)
XLA Ops:
  7.1 99.1 %first.1 = (bf16[2,1024,1024]{2,1,0:T(8,128)(2,1)}, bf16[2,1024,1024]{2,1,0:T(8,128)(2,1)}, bf16[2,1024,1024]{2,1,0:T(8,128)(2,1)}, bf16[1024,768]{1,0:T(8,128)(...) custom-call(bf16[1024,512]{1,0:T(8,128)(2,1)} %hidden.1, ...), custom_call_target="tpu_custom_call" | custom-call | tf_op jit(solution)/shard_map/first/pallas_call | solution.py:495
  106.2 3.4 convert_reduce_fusion.1
  114.9 4.6 fusion.9
  119.4 9.1 %feed.2 = (bf16[1024,1024]{1,0:T(8,128)(2,1)S(1)}, bf16[1024,1024]{1,0:T(8,128)(2,1)S(1)}, f32[1,1024]{1,0:T(1,128)S(1)}) custom-call(bf16[1024,1024]{1,0:T(8,128)(2,1)} %get-tuple-element.141.a_ref, bf16[1024,1024]{1,0:T(8,128)(2,1)} %get-tuple-element.145.g_ref, bf16[1024,1024]{1,0:T(8,128)(2,1)} %get-tuple-element.35.up_ref, ...), custom_call_target="tpu_custom_call" | custom-call | flops 4294967296 | bytes 12582912 | tf_op jit(solution)/shard_map/feed/pallas_call | solution.py:166
  128.6 4.4 fusion.68
  133.0 9.1 %feed.3 = (bf16[1024,1024]{1,0:T(8,128)(2,1)S(1)}, bf16[1024,1024]{1,0:T(8,128)(2,1)S(1)}, f32[1,1024]{1,0:T(1,128)S(1)}) custom-call(bf16[1024,1024]{1,0:T(8,128)(2,1)} %get-tuple-element.142.a_ref, bf16[1024,1024]{1,0:T(8,128)(2,1)} %get-tuple-element.146.g_ref, bf16[1024,1024]{1,0:T(8,128)(2,1)} %get-tuple-element.35.up_ref, ...), custom_call_target="tpu_custom_call" | custom-call | flops 4294967296 | bytes 12582912 | tf_op jit(solution)/shard_map/feed/pallas_call | solution.py:166
  142.1 5.6 %convolution_add_fusion = f32[1024,1024]{1,0:T(8,128)S(1)} fusion(f32[1024,1024]{1,0:T(8,128)} %fusion.68, bf16[1024,1024]{1,0:T(8,128)(2,1)S(1)} %get-tuple-element.38, bf16[2,1024,1024]{2,1,0:T(8,128)(2,1)S(1)} %copy-done.7), kind=kOutput, calls=%fused_computation.62 | convolution fusion | flops 2148532224 | bytes 12582912 | tf_op jit(solution)/shard_map/dot_general | solution.py:24
  153.3 2.6 convolution_add_fusion.1
  162.8 6.8 %fusion.75 = f32[1024,1024]{1,0:T(8,128)} fusion(bf16[1024,1024]{1,0:T(8,128)(2,1)} %copy-done.2, bf16[1024,1024]{1,0:T(8,128)(2,1)} %get-tuple-element.35.up_ref), kind=kOutput, calls=%fused_computation.190 | convolution fusion | flops 2147483648 | bytes 8388608 | tf_op jit(solution)/shard_map/dot_general | solution.py:24
  169.6 4.6 fusion.76
  174.1 6.7 %fusion.73 = f32[1024,1024]{1,0:T(8,128)} fusion(bf16[1024,1024]{1,0:T(8,128)(2,1)} %copy-done.3, bf16[1024,1024]{1,0:T(8,128)(2,1)} %get-tuple-element.36.down_ref), kind=kOutput, calls=%fused_computation.188 | convolution fusion | flops 2147483648 | bytes 8388608 | tf_op jit(solution)/shard_map/dot_general | solution.py:24
  180.9 4.3 fusion.74
  187.6 3.7 fusion.40
  194.7 9.4 %fusion.31 = (f32[1024]{0:T(1024)S(1)}, f32[1024]{0:T(1024)S(1)}, f32[1024]{0:T(1024)S(1)}, f32[1024]{0:T(1024)S(1)}, f32[1024]{0:T(1024)S(1)}, /*index=5*/f32[1...) fusion(f32[1024]{0:T(1024)S(1)} %add_rsqrt_fusion, ...), kind=kOutput, calls=%fused_computation.35 | convolution fusion | flops 1642057728 | bytes 28385280 | tf_op jit(solution)/shard_map/dot_general | solution.py:24
  204.2 6.4 %fusion.13 = (bf16[1024,1024]{1,0:T(8,128)(2,1)S(1)}, bf16[1024,1024]{1,0:T(8,128)(2,1)S(1)}) fusion(f32[1024,1024]{1,0:T(8,128)} %get-tuple-element.139, f32[1024]{0:T(1024)S(1)} %broadcast_multiply_fusion.2, f32[1024]{0:T(1024)S(1)} %broadcast_multiply_fusion.3, f32[1024]{0:T(1024)S(1)} %add_rsqrt_fusion.1, f32[1024]{0:T(1024)S(1)} %broadcast_multiply_fusion.5, ...), kind=kLoop, calls=%fused_computation.17 | loop fusion | flops 16777216 | bytes 16809984 | tf_op jit(solution)/shard_map/convert_element_type | solution.py:972
  224.0 3.4 collective-permute-start.15
  233.2 14.8 %collective-permute-done.17 = bf16[128,256]{1,0:T(8,128)(2,1)S(1)} collective-permute-done((bf16[128,256]{1,0:T(8,128)(2,1)S(1)}, bf16[128,256]{1,0:T(8,128)(2,1)S(1)}, u32[]{:S(2)}, u32[]{:S(2)}) %collective-permute-start.17) | collective-permute-done | bytes 65568 | tf_op jit(solution)/shard_map/ppermute | solution.py:789
  255.3 3.0 collective-permute-done.10
  258.3 3.4 collective-permute-done.8
  261.7 5.4 %collective-permute-done.9 = bf16[256,384]{0,1:T(8,128)(2,1)S(1)} collective-permute-done((bf16[256,384]{0,1:T(8,128)(2,1)S(1)}, bf16[256,384]{0,1:T(8,128)(2,1)S(1)}, u32[]{:S(2)}, u32[]{:S(2)}) %collective-permute-start.9) | collective-permute-done | bytes 196640 | tf_op jit(solution)/shard_map/ppermute | solution.py:792
  270.2 3.0 collective-permute-start.27
  281.3 2.6 collective-permute-start.22
  283.9 11.0 %collective-permute-done.27 = bf16[512,256]{1,0:T(8,128)(2,1)S(1)} collective-permute-done((bf16[512,256]{1,0:T(8,128)(2,1)S(1)}, bf16[512,256]{1,0:T(8,128)(2,1)S(1)}, u32[]{:S(2)}, u32[]{:S(2)}) %collective-permute-start.27) | collective-permute-done | bytes 262176 | tf_op jit(solution)/shard_map/ppermute | solution.py:792
  298.1 12.4 %collective-permute-done.21 = bf16[256,512]{0,1:T(8,128)(2,1)S(1)} collective-permute-done((bf16[256,512]{0,1:T(8,128)(2,1)S(1)}, bf16[256,512]{0,1:T(8,128)(2,1)S(1)}, u32[]{:S(2)}, u32[]{:S(2)}) %collective-permute-start.21) | collective-permute-done | bytes 262176 | tf_op jit(solution)/shard_map/ppermute | solution.py:792
  315.1 3.0 copy.66
  322.1 5.0 %collective-permute-done.23 = bf16[256,512]{0,1:T(8,128)(2,1)S(1)} collective-permute-done((bf16[256,512]{0,1:T(8,128)(2,1)S(1)}, bf16[256,512]{0,1:T(8,128)(2,1)S(1)}, u32[]{:S(2)}, u32[]{:S(2)}) %collective-permute-start.23) | collective-permute-done | bytes 262176 | tf_op jit(solution)/shard_map/ppermute | solution.py:789
  329.3 7.6 %collective-permute-done.5 = bf16[1024,512]{1,0:T(8,128)(2,1)} collective-permute-done((bf16[1024,512]{1,0:T(8,128)(2,1)}, bf16[1024,512]{1,0:T(8,128)(2,1)}, u32[]{:S(2)}, u32[]{:S(2)}) %collective-permute-start.5) | collective-permute-done | bytes 1048608 | tf_op jit(solution)/shard_map/ppermute | solution.py:785
  336.9 3.4 convert_reduce_fusion.5
  340.3 40.4 %collective-permute-done.24 = bf16[256,1024]{0,1:T(8,128)(2,1)S(1)} collective-permute-done((bf16[256,1024]{0,1:T(8,128)(2,1)S(1)}, bf16[256,1024]{0,1:T(8,128)(2,1)S(1)}, u32[]{:S(2)}, u32[]{:S(2)}) %collective-permute-start.24) | collective-permute-done | bytes 524320 | tf_op jit(solution)/shard_map/ppermute | solution.py:785
  381.7 79.6 %psum.7 = f32[6144]{0:T(1024)S(1)} all-reduce(f32[6144]{0:T(1024)S(1)} %constant_dynamic-update-slice_fusion), channel_id=1, replica_groups=mesh['dp'=4,'row'=4,'col'=2] {'dp','row'}, use_global_device_ids=true, to_apply=%region_20.21 | all-reduce | flops 6144 | bytes 49152 | tf_op jit(solution)/shard_map/psum | solution.py:1004
  464.4 2.9 copy.67
  471.4 3.5 add_add_fusion
  (256 shorter events, 89.7 us)
Async XLA Ops:
  128.5 21.8 %copy-start.2 = (bf16[1024,1024]{1,0:T(8,128)(2,1)}, bf16[1024,1024]{1,0:T(8,128)(2,1)S(1)}, u32[]{:S(2)}) copy-start(bf16[1024,1024]{1,0:T(8,128)(2,1)S(1)} %get-tuple-element.41) | copy-start | bytes 6291460
  148.9 119.4 %collective-permute-start.25 = (bf16[512,1024]{1,0:T(8,128)(2,1)}, bf16[512,1024]{1,0:T(8,128)(2,1)}, u32[]{:S(2)}, u32[]{:S(2)}) collective-permute-start(bf16[512,1024]{1,0:T(8,128)(2,1)} %slice.267), channel_id=1, source_target_pairs={{0,16},{8,24},{16,0},{24,8},{1,17},{9,25},{17,1},{25,9},{2,18},{10... | collective-permute-start | bytes 3145736 | tf_op jit(solution)/shard_map/ppermute | solution.py:789
  157.2 113.0 %collective-permute-start.19 = (bf16[1024,512]{0,1:T(8,128)(2,1)}, bf16[1024,512]{0,1:T(8,128)(2,1)}, u32[]{:S(2)}, u32[]{:S(2)}) collective-permute-start(bf16[1024,512]{0,1:T(8,128)(2,1)} %slice.268), channel_id=1, source_target_pairs={{0,16},{8,24},{16,0},{24,8},{1,17},{9,25},{17,1},{25,9},{2,18},{10... | collective-permute-start | bytes 3145736 | tf_op jit(solution)/shard_map/ppermute | solution.py:789
  162.0 61.3 %collective-permute-start.13 = (bf16[128,1024]{1,0:T(8,128)(2,1)}, bf16[128,1024]{1,0:T(8,128)(2,1)S(1)}, u32[]{:S(2)}, u32[]{:S(2)}) collective-permute-start(bf16[128,1024]{1,0:T(8,128)(2,1)} %slice.270), channel_id=1, source_target_pairs={{0,16},{8,24},{16,0},{24,8},{1,17},{9,25},{17,1},{25,9},{2,18},{10... | collective-permute-start | bytes 786440 | tf_op jit(solution)/shard_map/ppermute | solution.py:789
  223.4 6.6 %collective-permute-start.14 = (bf16[128,256]{1,0:T(8,128)(2,1)S(1)}, bf16[128,256]{1,0:T(8,128)(2,1)S(1)}, u32[]{:S(2)}, u32[]{:S(2)}) collective-permute-start(bf16[128,256]{1,0:T(8,128)(2,1)S(1)} %get-tuple-element.168), channel_id=1, source_target_pairs={{0,2},{2,4},{4,6},{6,0},{1,3},{3,5},{5,7},{7,1},{8,10},{10,12},{12... | collective-permute-start | bytes 196616 | tf_op jit(solution)/shard_map/ppermute | solution.py:792
  224.0 7.3 %collective-permute-start.15 = (bf16[128,256]{1,0:T(8,128)(2,1)S(1)}, bf16[128,256]{1,0:T(8,128)(2,1)S(1)}, u32[]{:S(2)}, u32[]{:S(2)}) collective-permute-start(bf16[128,256]{1,0:T(8,128)(2,1)S(1)} %get-tuple-element.170), channel_id=1, source_target_pairs={{0,4},{2,6},{4,0},{6,2},{1,5},{3,7},{5,1},{7,3},{8,12},{10,14},{12... | collective-permute-start | bytes 196616 | tf_op jit(solution)/shard_map/ppermute | solution.py:792
  227.5 4.6 collective-permute-start.16
  230.0 19.6 %collective-permute-start.7 = (bf16[1024,384]{0,1:T(8,128)(2,1)}, bf16[1024,384]{0,1:T(8,128)(2,1)S(1)}, u32[]{:S(2)}, u32[]{:S(2)}) collective-permute-start(bf16[1024,384]{0,1:T(8,128)(2,1)} %slice.269), channel_id=1, source_target_pairs={{0,16},{8,24},{16,0},{24,8},{1,17},{9,25},{17,1},{25,9},{2,18},{10... | collective-permute-start | bytes 2359304 | tf_op jit(solution)/shard_map/ppermute | solution.py:789
  231.4 1.9 collective-permute-start.6
  232.1 15.9 %collective-permute-start.17 = (bf16[128,256]{1,0:T(8,128)(2,1)S(1)}, bf16[128,256]{1,0:T(8,128)(2,1)S(1)}, u32[]{:S(2)}, u32[]{:S(2)}) collective-permute-start(bf16[128,256]{1,0:T(8,128)(2,1)S(1)} %add_convert_fusion.7), channel_id=1, source_target_pairs={{0,16},{8,24},{16,0},{24,8},{1,17},{9,25},{17,1},{25,9},{2,18},{10... | collective-permute-start | bytes 196616 | tf_op jit(solution)/shard_map/ppermute | solution.py:789
  248.1 5.5 %collective-permute-start.18 = (bf16[256,256]{1,0:T(8,128)(2,1)S(1)}, bf16[256,256]{1,0:T(8,128)(2,1)S(1)}, u32[]{:S(2)}, u32[]{:S(2)}) collective-permute-start(bf16[256,256]{1,0:T(8,128)(2,1)S(1)} %pad_maximum_fusion.5), channel_id=1, source_target_pairs={{0,8},{8,0},{16,24},{24,16},{1,9},{9,1},{17,25},{25,17},{2,10},{10... | collective-permute-start | bytes 393224 | tf_op jit(solution)/shard_map/ppermute | solution.py:785
  251.5 6.7 %collective-permute-start.10 = (bf16[256,384]{0,1:T(8,128)(2,1)S(1)}, bf16[256,384]{0,1:T(8,128)(2,1)S(1)}, u32[]{:S(2)}, u32[]{:S(2)}) collective-permute-start(bf16[256,384]{0,1:T(8,128)(2,1)S(1)} %get-tuple-element.154), channel_id=1, source_target_pairs={{0,6},{2,0},{4,2},{6,4},{1,7},{3,1},{5,3},{7,5},{8,14},{10,8},{12,... | collective-permute-start | bytes 589832 | tf_op jit(solution)/shard_map/ppermute | solution.py:792
  253.1 8.6 %collective-permute-start.8 = (bf16[256,384]{0,1:T(8,128)(2,1)S(1)}, bf16[256,384]{0,1:T(8,128)(2,1)S(1)}, u32[]{:S(2)}, u32[]{:S(2)}) collective-permute-start(bf16[256,384]{0,1:T(8,128)(2,1)S(1)} %get-tuple-element.153), channel_id=1, source_target_pairs={{0,2},{2,4},{4,6},{6,0},{1,3},{3,5},{5,7},{7,1},{8,10},{10,12},{12... | collective-permute-start | bytes 589832 | tf_op jit(solution)/shard_map/ppermute | solution.py:792
  253.6 13.5 %collective-permute-start.9 = (bf16[256,384]{0,1:T(8,128)(2,1)S(1)}, bf16[256,384]{0,1:T(8,128)(2,1)S(1)}, u32[]{:S(2)}, u32[]{:S(2)}) collective-permute-start(bf16[256,384]{0,1:T(8,128)(2,1)S(1)} %get-tuple-element.155), channel_id=1, source_target_pairs={{0,4},{2,6},{4,0},{6,2},{1,5},{3,7},{5,1},{7,3},{8,12},{10,14},{12... | collective-permute-start | bytes 589832 | tf_op jit(solution)/shard_map/ppermute | solution.py:792
  258.3 17.0 %collective-permute-start.4 = (bf16[1024,512]{1,0:T(8,128)(2,1)S(1)}, bf16[1024,512]{1,0:T(8,128)(2,1)S(1)}, u32[]{:S(2)}, u32[]{:S(2)}) collective-permute-start(bf16[1024,512]{1,0:T(8,128)(2,1)S(1)} %copy-done.30), channel_id=1, source_target_pairs={{0,1},{1,0},{2,3},{3,2},{4,5},{5,4},{6,7},{7,6},{8,9},{9,8},{10,11... | collective-permute-start | bytes 3145736 | tf_op jit(solution)/shard_map/ppermute | solution.py:795
  261.7 15.7 %collective-permute-start.1 = (bf16[1024,512]{1,0:T(8,128)(2,1)S(1)}, bf16[1024,512]{1,0:T(8,128)(2,1)S(1)}, u32[]{:S(2)}, u32[]{:S(2)}) collective-permute-start(bf16[1024,512]{1,0:T(8,128)(2,1)S(1)} %copy-done.29), channel_id=1, source_target_pairs={{0,1},{1,0},{2,3},{3,2},{4,5},{5,4},{6,7},{7,6},{8,9},{9,8},{10,11... | collective-permute-start | bytes 3145736 | tf_op jit(solution)/shard_map/ppermute | solution.py:795
  267.2 12.9 %collective-permute-start.11 = (bf16[256,384]{0,1:T(8,128)(2,1)S(1)}, bf16[256,384]{0,1:T(8,128)(2,1)S(1)}, u32[]{:S(2)}, u32[]{:S(2)}) collective-permute-start(bf16[256,384]{0,1:T(8,128)(2,1)S(1)} %add_convert_fusion.6), channel_id=1, source_target_pairs={{0,16},{8,24},{16,0},{24,8},{1,17},{9,25},{17,1},{25,9},{2,18},{10... | collective-permute-start | bytes 589832 | tf_op jit(solution)/shard_map/ppermute | solution.py:789
  270.1 11.1 %collective-permute-start.26 = (bf16[512,256]{1,0:T(8,128)(2,1)S(1)}, bf16[512,256]{1,0:T(8,128)(2,1)S(1)}, u32[]{:S(2)}, u32[]{:S(2)}) collective-permute-start(bf16[512,256]{1,0:T(8,128)(2,1)S(1)} %get-tuple-element.147), channel_id=1, source_target_pairs={{0,2},{2,4},{4,6},{6,0},{1,3},{3,5},{5,7},{7,1},{8,10},{10,12},{12... | collective-permute-start | bytes 786440 | tf_op jit(solution)/shard_map/ppermute | solution.py:792
  270.2 24.7 %collective-permute-start.27 = (bf16[512,256]{1,0:T(8,128)(2,1)S(1)}, bf16[512,256]{1,0:T(8,128)(2,1)S(1)}, u32[]{:S(2)}, u32[]{:S(2)}) collective-permute-start(bf16[512,256]{1,0:T(8,128)(2,1)S(1)} %get-tuple-element.149), channel_id=1, source_target_pairs={{0,4},{2,6},{4,0},{6,2},{1,5},{3,7},{5,1},{7,3},{8,12},{10,14},{12... | collective-permute-start | bytes 786440 | tf_op jit(solution)/shard_map/ppermute | solution.py:792
  275.2 19.7 %collective-permute-start.28 = (bf16[512,256]{1,0:T(8,128)(2,1)S(1)}, bf16[512,256]{1,0:T(8,128)(2,1)S(1)}, u32[]{:S(2)}, u32[]{:S(2)}) collective-permute-start(bf16[512,256]{1,0:T(8,128)(2,1)S(1)} %get-tuple-element.148), channel_id=1, source_target_pairs={{0,6},{2,0},{4,2},{6,4},{1,7},{3,1},{5,3},{7,5},{8,14},{10,8},{12,... | collective-permute-start | bytes 786440 | tf_op jit(solution)/shard_map/ppermute | solution.py:792
  277.5 20.6 %collective-permute-start.20 = (bf16[256,512]{0,1:T(8,128)(2,1)S(1)}, bf16[256,512]{0,1:T(8,128)(2,1)S(1)}, u32[]{:S(2)}, u32[]{:S(2)}) collective-permute-start(bf16[256,512]{0,1:T(8,128)(2,1)S(1)} %get-tuple-element.150), channel_id=1, source_target_pairs={{0,2},{2,4},{4,6},{6,0},{1,3},{3,5},{5,7},{7,1},{8,10},{10,12},{12... | collective-permute-start | bytes 786440 | tf_op jit(solution)/shard_map/ppermute | solution.py:792
  280.1 30.4 %collective-permute-start.21 = (bf16[256,512]{0,1:T(8,128)(2,1)S(1)}, bf16[256,512]{0,1:T(8,128)(2,1)S(1)}, u32[]{:S(2)}, u32[]{:S(2)}) collective-permute-start(bf16[256,512]{0,1:T(8,128)(2,1)S(1)} %get-tuple-element.152), channel_id=1, source_target_pairs={{0,4},{2,6},{4,0},{6,2},{1,5},{3,7},{5,1},{7,3},{8,12},{10,14},{12... | collective-permute-start | bytes 786440 | tf_op jit(solution)/shard_map/ppermute | solution.py:792
  281.3 30.3 %collective-permute-start.22 = (bf16[256,512]{0,1:T(8,128)(2,1)S(1)}, bf16[256,512]{0,1:T(8,128)(2,1)S(1)}, u32[]{:S(2)}, u32[]{:S(2)}) collective-permute-start(bf16[256,512]{0,1:T(8,128)(2,1)S(1)} %get-tuple-element.151), channel_id=1, source_target_pairs={{0,6},{2,0},{4,2},{6,4},{1,7},{3,1},{5,3},{7,5},{8,14},{10,8},{12,... | collective-permute-start | bytes 786440 | tf_op jit(solution)/shard_map/ppermute | solution.py:792
  294.9 33.4 %collective-permute-start.3 = (bf16[1024,512]{1,0:T(8,128)(2,1)}, bf16[1024,512]{1,0:T(8,128)(2,1)}, u32[]{:S(2)}, u32[]{:S(2)}) collective-permute-start(bf16[1024,512]{1,0:T(8,128)(2,1)} %constant_dynamic-slice_fusion.2), channel_id=1, source_target_pairs={{0,1},{1,0},{2,3},{3,2},{4,5},{5,4},{6,7},{7,6},{8,9},{9,8},{10,11... | collective-permute-start | bytes 3145736 | tf_op jit(solution)/shard_map/ppermute | solution.py:795
  294.9 17.8 %collective-permute-start.12 = (bf16[256,768]{0,1:T(8,128)(2,1)S(1)}, bf16[256,768]{0,1:T(8,128)(2,1)S(1)}, u32[]{:S(2)}, u32[]{:S(2)}) collective-permute-start(bf16[256,768]{0,1:T(8,128)(2,1)S(1)} %pad_maximum_fusion.4), channel_id=1, source_target_pairs={{0,8},{8,0},{16,24},{24,16},{1,9},{9,1},{17,25},{25,17},{2,10},{10... | collective-permute-start | bytes 1179656 | tf_op jit(solution)/shard_map/ppermute | solution.py:785
  298.1 173.3 %collective-permute-start = (bf16[1024,512]{1,0:T(8,128)(2,1)}, bf16[1024,512]{1,0:T(8,128)(2,1)}, u32[]{:S(2)}, u32[]{:S(2)}) collective-permute-start(bf16[1024,512]{1,0:T(8,128)(2,1)} %constant_dynamic-slice_fusion.4), channel_id=1, source_target_pairs={{0,1},{1,0},{2,3},{3,2},{4,5},{5,4},{6,7},{7,6},{8,9},{9,8},{10,11... | collective-permute-start | bytes 3145736 | tf_op jit(solution)/shard_map/ppermute | solution.py:795
  310.5 26.4 %collective-permute-start.5 = (bf16[1024,512]{1,0:T(8,128)(2,1)}, bf16[1024,512]{1,0:T(8,128)(2,1)}, u32[]{:S(2)}, u32[]{:S(2)}) collective-permute-start(bf16[1024,512]{1,0:T(8,128)(2,1)} %add_convert_fusion.2), channel_id=1, source_target_pairs={{0,8},{8,0},{16,24},{24,16},{1,9},{9,1},{17,25},{25,17},{2,10},{10... | collective-permute-start | bytes 3145736 | tf_op jit(solution)/shard_map/ppermute | solution.py:785
  311.6 159.8 %collective-permute-start.2 = (bf16[1024,512]{1,0:T(8,128)(2,1)}, bf16[1024,512]{1,0:T(8,128)(2,1)}, u32[]{:S(2)}, u32[]{:S(2)}) collective-permute-start(bf16[1024,512]{1,0:T(8,128)(2,1)} %add_convert_fusion.3), channel_id=1, source_target_pairs={{0,8},{8,0},{16,24},{24,16},{1,9},{9,1},{17,25},{25,17},{2,10},{10... | collective-permute-start | bytes 3145736 | tf_op jit(solution)/shard_map/ppermute | solution.py:785
  312.7 7.6 %collective-permute-start.29 = (bf16[512,256]{1,0:T(8,128)(2,1)S(1)}, bf16[512,256]{1,0:T(8,128)(2,1)S(1)}, u32[]{:S(2)}, u32[]{:S(2)}) collective-permute-start(bf16[512,256]{1,0:T(8,128)(2,1)S(1)} %add_convert_fusion.4), channel_id=1, source_target_pairs={{0,16},{8,24},{16,0},{24,8},{1,17},{9,25},{17,1},{25,9},{2,18},{10... | collective-permute-start | bytes 786440 | tf_op jit(solution)/shard_map/ppermute | solution.py:789
  320.3 6.8 %collective-permute-start.23 = (bf16[256,512]{0,1:T(8,128)(2,1)S(1)}, bf16[256,512]{0,1:T(8,128)(2,1)S(1)}, u32[]{:S(2)}, u32[]{:S(2)}) collective-permute-start(bf16[256,512]{0,1:T(8,128)(2,1)S(1)} %add_convert_fusion.5), channel_id=1, source_target_pairs={{0,16},{8,24},{16,0},{24,8},{1,17},{9,25},{17,1},{25,9},{2,18},{10... | collective-permute-start | bytes 786440 | tf_op jit(solution)/shard_map/ppermute | solution.py:789
  327.1 141.6 %collective-permute-start.30 = (bf16[1024,256]{1,0:T(8,128)(2,1)}, bf16[1024,256]{1,0:T(8,128)(2,1)}, u32[]{:S(2)}, u32[]{:S(2)}) collective-permute-start(bf16[1024,256]{1,0:T(8,128)(2,1)} %pad_maximum_fusion.2), channel_id=1, source_target_pairs={{0,8},{8,0},{16,24},{24,16},{1,9},{9,1},{17,25},{25,17},{2,10},{10... | collective-permute-start | bytes 1572872 | tf_op jit(solution)/shard_map/ppermute | solution.py:785
  328.3 52.4 %collective-permute-start.24 = (bf16[256,1024]{0,1:T(8,128)(2,1)S(1)}, bf16[256,1024]{0,1:T(8,128)(2,1)S(1)}, u32[]{:S(2)}, u32[]{:S(2)}) collective-permute-start(bf16[256,1024]{0,1:T(8,128)(2,1)S(1)} %pad_maximum_fusion.1), channel_id=1, source_target_pairs={{0,8},{8,0},{16,24},{24,16},{1,9},{9,1},{17,25},{25,17},{2,10},{10... | collective-permute-start | bytes 1572872 | tf_op jit(solution)/shard_map/ppermute | solution.py:785
  (45 other events, 232.7 us)

commit v3 on v2

--- a/solution.py
+++ b/solution.py
@@ -272,10 +272,11 @@
     mix[:, cols[2]] = dv_acc[...].astype(BF16)
 
 
-def first_kernel(
-    hidden, cot, wq_in, wo_in, wu_in, wd_in, rows_in, params_in, bq_in, freq_in,
-    x_out, g_out, a_out, wq_out, wo_out, wu_out, wd_out, mix_out, ctx_out, rows_out, params_out,
-    X, G, A, WQ, WO, WU, WD, MIX, GC, CTX, rows_far, params, seg_col, cos_tab, sin_tab, dk_acc, dv_acc,
+def block_kernel(
+    hidden, cot, wq_in, wo_in, wu_in, wd_in, rows_in, params_in, bq_in, bu_in, freq_in,
+    rq_out, ro_out, ru_out, rd_out, keep_out, near_out, far_out, small_out,
+    X, G, A, WQ, WO, WU, WD, MIX, GC, CTX, ACT, GUP, rows_far, params, seg_col, cos_tab, sin_tab, dk_acc, dv_acc,
+    SQ, SO, SU, SD, YQ, YO, YU, YD, ZQ, ZO, ZU, ZD, HQ, HO, HU, HD, RQ, RO, RU, RD, LAND, SMALL, SMALL_Z, SMALL_P,
     send_sems, recv_sems, local_sems, *, rows_n,
 ):
     R = rows_n
@@ -461,48 +462,249 @@
     pull_context(1)
     for pair in range(pairs):
         attend(1, rows_far, pair)
+    everything = pl.ds(0, length)
+    grads = {
+        "q": (SQ, YQ, ZQ, HQ, RQ, rq_out, lambda t: (block(t), slice(None)), lambda q: (slice(None), pl.ds(q * qc, qc))),
+        "o": (SO, YO, ZO, HO, RO, ro_out, lambda t: (slice(None), block(t)), lambda q: (pl.ds(q * oc, oc), slice(None))),
+        "u": (SU, YU, ZU, HU, RU, ru_out, lambda t: (block(t), slice(None)), lambda q: (slice(None), pl.ds(q * uc, uc))),
+        "d": (SD, YD, ZD, HD, RD, rd_out, lambda t: (slice(None), block(t)), lambda q: (pl.ds(q * uc, uc), slice(None))),
+    }
+
+    def multiply(name, h, t):
+        if name == "q":
+            pairs_of = [(A[s, :, block(t)], MIX[s, :, pl.ds(h * qc, qc)]) for s in range(2)]
+        elif name == "u":
+            pairs_of = [(A[s, :, block(t)], GUP[s, :, pl.ds(h * uc, uc)]) for s in range(2)]
+        elif name == "o":
+            pairs_of = [(CTX[s, :, pl.ds(h * oc, oc)], G[s, :, block(t)]) for s in range(2)]
+        else:
+            pairs_of = [(ACT[s, :, pl.ds(h * uc, uc)], G[s, :, block(t)]) for s in range(2)]
+        return (dot(*pairs_of[0], TN) + dot(*pairs_of[1], TN)).astype(BF16)
+
+    turns = list(range(1, R)) + [0]
+
+    def other_part(name):
+        source, landed, _, _, _, _, spot, _ = grads[name]
+        for t in turns:
+            source[spot(t)] = multiply(name, 1, t)
+            net.send(("gy", name, t), source.at[spot(t)], landed.at[spot(t)], ydev)
+
+    def own_part(name):
+        kept, spot = grads[name][2], grads[name][6]
+
+        @pl.loop(0, R)
+        def _(t):
+            kept[spot(t)] = multiply(name, 0, t)
+
+    def across(name):
+        _, landed, kept, hops, _, _, spot, _ = grads[name]
+        for t in turns:
+            net.wait(("gy", name, t), landed.at[spot(t)], ydev)
+            kept[spot(t)] = (kept[spot(t)].astype(F32) + landed[spot(t)].astype(F32)).astype(BF16)
+            if t:
+                net.send(("gz", name, t), kept.at[spot(t)], hops.at[t - 1], zdev(t))
+
+    def finish(name):
+        _, _, kept, hops, result, _, spot, seat = grads[name]
+        total = kept[spot(0)].astype(F32)
+        for t in range(1, R):
+            net.wait(("gz", name, t), hops.at[t - 1], zdev(-t))
+            total = total + hops[t - 1].astype(F32)
+        spot_here = seat(side * 2 + quarter)
+        result[spot_here] = total.astype(BF16)
+        net.send(("ry", name), result.at[spot_here], result.at[spot_here], ydev)
+        net.send(("rx", name), result.at[spot_here], result.at[spot_here], xdev)
+
+    def spread_out(name):
+        result, seat = grads[name][4], grads[name][7]
+        spot_y = seat(side * 2 + 1 - quarter)
+        net.wait(("ry", name), result.at[spot_y], ydev)
+        net.send(("rxy", name), result.at[spot_y], result.at[spot_y], xdev)
+
+    def collect(name):
+        result, seat = grads[name][4], grads[name][7]
+        net.wait(("rx", name), result.at[seat((1 - side) * 2 + quarter)], xdev)
+        net.wait(("rxy", name), result.at[seat((1 - side) * 2 + 1 - quarter)], xdev)
+        return move(result, grads[name][5])
+
+    SMALL[...] = jnp.zeros_like(SMALL)
+    for name in "oq":
+        other_part(name)
+    for name in "oq":
+        own_part(name)
+    for h in range(2):
+        sums = [jnp.sum(MIX[s, :, pl.ds(h * qc, qc)].astype(F32), axis=0, keepdims=True) for s in range(2)]
+        seat = quarter if h == 0 else 1 - quarter
+        SMALL[0:1, pl.ds(pl.multiple_of(seat * qc, LANES), qc)] = sums[0] + sums[1]
+
     arrive("u")
     arrive("d")
+    for s in range(2):
+        each_tile(lambda at: norm(s, at, 2, 3))
+
+    def feed_part(s, h):
+        seat = quarter if h == 0 else 1 - quarter
+
+        def body(at):
+            for begin in range(0, uc, tile):
+                cols = pl.ds(h * uc + begin, tile)
+                up = dot(A[s, at, :], WU[:, cols]) + bu_in[:, cols]
+                pull = dot(G[s, at, :], WD[cols, :], NT)
+                gate = 0.5 * (1.0 + lax.erf(up * 0.5**0.5))
+                bell = jnp.exp(-0.5 * up * up) * 0.3989422804014327
+                ACT[s, at, cols] = (up * gate).astype(BF16)
+                grad = (pull * (gate + up * bell)).astype(BF16)
+                GUP[s, at, cols] = grad
+                SMALL[1:2, pl.ds(pl.multiple_of(seat * uc + begin, tile), tile)] += jnp.sum(
+                    grad.astype(F32), axis=0, keepdims=True
+                )
+
+        each_tile(body)
+
+    for s in range(2):
+        feed_part(s, 1)
+    for name in "du":
+        other_part(name)
+    for name in "oq":
+        across(name)
+    for s in range(2):
+        feed_part(s, 0)
+    for name in "du":
+        own_part(name)
+
+    def leave(s, c):
+        @pl.loop(0, piece // tile)
+        def _(i):
+            at = pl.ds(pl.multiple_of(c * piece + i * tile, tile), tile)
+            result = dot(CTX[s, at, :], WO[...]) + dot(ACT[s, at, :], WD[...])
+            ACT[s, at, :] = result.astype(BF16)
+            grad_one = dot(MIX[s, at, :], WQ[...], NT)
+            grad_two = dot(GUP[s, at, :], WU[...], NT)
+            values = X[s, at, :].astype(F32)
+            centred = values - jnp.mean(values, axis=-1, keepdims=True)
+            inv = lax.rsqrt(jnp.mean(centred * centred, axis=-1, keepdims=True) + EPS)
+            unit = centred * inv
+            for i_row, value in enumerate([grad_one * unit, grad_one, grad_two * unit, grad_two]):
+                SMALL[2 + i_row : 3 + i_row, :] += jnp.sum(value, axis=0, keepdims=True)
+            scaled = grad_one * params[0:1, :] + grad_two * params[2:3, :]
+            mean_scaled = jnp.mean(scaled, axis=1, keepdims=True)
+            mean_unit = jnp.mean(scaled * unit, axis=1, keepdims=True)
+            GUP[s, at, :] = (inv * (scaled - mean_scaled - unit * mean_unit)).astype(BF16)
+            if s == 0:
+                SMALL[6:7, own_cols] += jnp.sum(G[0, at, own_cols].astype(F32), axis=0, keepdims=True)
+
+        span = pl.ds(c * piece, piece)
+        for i, buffer in enumerate([ACT, GUP]):
+            if s == 1:
+                net.send(("out", i, c), buffer.at[1, span, far_cols], LAND.at[i, span, :], core)
+            else:
+                net.send(("own out", i, c), buffer.at[0, span, far_cols], near_out.at[i, span, :], core)
+
+    def leave_far(c):
+        span = pl.ds(c * piece, piece)
+        for i, buffer in enumerate([ACT, GUP]):
+            net.wait(("out", i, c), LAND.at[i, span, :], core)
+            LAND[i, span, :] = (LAND[i, span, :].astype(F32) + buffer[1, span, own_cols].astype(F32)).astype(BF16)
+            net.send(("far out", i, c), LAND.at[i, span, :], far_out.at[i, span, :], xdev)
+
+    leave(1, 0)
+    leave(1, 1)
+    leave_far(0)
+    for name in "d":
+        across(name)
+    leave_far(1)
+    for name in "oq":
+        finish(name)
+    leave(0, 0)
+    for name in "oq":
+        spread_out(name)
+    leave(0, 1)
+    kept_copies = [move(ACT.at[0, :, own_cols], keep_out.at[0]), move(GUP.at[0, :, own_cols], keep_out.at[1])]
+
+    for t in range(1, R):
+        net.send(("sz", t), SMALL, SMALL_Z.at[row], zdev(t))
+    across("u")
+    finish("d")
+    SMALL_Z[row] = SMALL[...]
+    for t in range(1, R):
+        net.wait(("sz", t), SMALL_Z.at[lax.rem(row - t + R, R)], zdev(-t))
+    total = SMALL_Z[0]
+    for r in range(1, R):
+        total = total + SMALL_Z[r]
+    SMALL_P[0] = total
+    net.send("sy", SMALL_P.at[0], SMALL_P.at[1], ydev)
+    spread_out("d")
+    finish("u")
+    net.wait("sy", SMALL_P.at[1], ydev)
+    SMALL_P[2] = SMALL_P[0] + SMALL_P[1]
+    net.send("sx", SMALL_P.at[2], SMALL_P.at[3], xdev)
+    done = [collect(name) for name in "oq"]
+    net.wait("sx", SMALL_P.at[3], xdev)
+    SMALL_P[4] = SMALL_P[2] + SMALL_P[3]
+    net.send("sc", SMALL_P.at[4], SMALL_P.at[5], core)
+    spread_out("u")
+    net.wait("sc", SMALL_P.at[5], core)
+    SMALL_P[5] = SMALL_P[4] + SMALL_P[5]
+    done += [
+        move(SMALL_P.at[2], small_out.at[side]),
+        move(SMALL_P.at[3], small_out.at[1 - side]),
+        move(SMALL_P.at[4], small_out.at[2]),
+        move(SMALL_P.at[5], small_out.at[3]),
+    ]
+    for c in range(chunks):
+        span = pl.ds(c * piece, piece)
+        for i in range(2):
+            net.wait(("own out", i, c), near_out.at[i, span, :], core)
+            net.wait(("far out", i, c), far_out.at[i, span, :], xdev)
+    done += [collect(name) for name in "du"]
+    for copy in kept_copies + done:
+        copy.wait()
     net.drain()
-    done = [
-        move(a, b)
-        for a, b in [
-            (X, x_out), (G, g_out), (A, a_out), (WQ, wq_out), (WO, wo_out), (WU, wu_out), (WD, wd_out),
-            (MIX, mix_out), (CTX, ctx_out), (rows_far, rows_out), (params, params_out),
-        ]
-    ]
-    for copy in done:
-        copy.wait()
-
-
-def first(hidden, cot, wq, wo, wu, wd, rows, params, bq, freq, rows_n):
+
+
+def whole_block(hidden, cot, wq, wo, wu, wd, rows, params, bq, bu, freq, rows_n):
     length, half = hidden.shape
     width = 2 * half
+    shard = wq.shape[0]
     wide3 = wq.shape[1]
     wide = wide3 // 3
     units = wu.shape[1] // 2
-    arrays = [
-        ((2, length, width), BF16), ((2, length, width), BF16), ((2, length, width), BF16),
-        ((width, wide3), BF16), ((wide, width), BF16), ((width, units), BF16), ((units, width), BF16),
-        ((2, length, wide3), BF16), ((2, length, wide), BF16), (rows.shape, F32), ((params.shape[0], width), F32),
+    qc, oc, uc = wide3 // 2, wide // 2, units // 2
+    out_shape = [
+        jax.ShapeDtypeStruct(shape, kind)
+        for shape, kind in [
+            ((shard, 4 * qc), BF16), ((4 * oc, shard), BF16), ((shard, 4 * uc), BF16), ((4 * uc, shard), BF16),
+            ((2, length, half), BF16), ((2, length, half), BF16), ((2, length, half), BF16), ((4, 8, width), F32),
+        ]
     ]
-    out_shape = [jax.ShapeDtypeStruct(shape, kind) for shape, kind in arrays]
-    buffers = [pltpu.VMEM(shape, kind) for shape, kind in arrays]
-    buffers.insert(8, pltpu.VMEM((length, wide), BF16))
-    table = pltpu.VMEM((length, LANES), F32)
+    both = lambda n, kind=BF16: pltpu.VMEM((2, length, n), kind)
+    plain = lambda *shape: pltpu.VMEM(shape, BF16)
+    floats = lambda *shape: pltpu.VMEM(shape, F32)
+    quarter_grads = [plain(width, qc), plain(oc, width), plain(width, uc), plain(uc, width)]
+    scratch = [
+        both(width), both(width), both(width),
+        plain(width, wide3), plain(wide, width), plain(width, units), plain(units, width),
+        both(wide3), plain(length, wide), both(wide), both(units), both(units),
+        floats(*rows.shape), floats(params.shape[0], width),
+        *[floats(length, LANES)] * 5,
+        *quarter_grads * 3,
+        plain(rows_n - 1, shard, qc), plain(rows_n - 1, oc, shard), plain(rows_n - 1, shard, uc), plain(rows_n - 1, uc, shard),
+        plain(shard, 4 * qc), plain(4 * oc, shard), plain(shard, 4 * uc), plain(4 * uc, shard),
+        both(half), floats(8, width), floats(rows_n, 8, width), floats(6, 8, width),
+    ]
     any_spec = pl.BlockSpec(memory_space=pl.ANY)
     vmem_spec = pl.BlockSpec(memory_space=pltpu.VMEM)
     return pl.pallas_call(
-        functools.partial(first_kernel, rows_n=rows_n),
+        functools.partial(block_kernel, rows_n=rows_n),
         out_shape=out_shape,
-        in_specs=[any_spec] * 6 + [vmem_spec] * 4,
+        in_specs=[any_spec] * 6 + [vmem_spec] * 5,
         out_specs=[any_spec] * len(out_shape),
-        scratch_shapes=buffers + [table] * 5 + [
-            pltpu.SemaphoreType.DMA((80,)), pltpu.SemaphoreType.DMA((80,)), pltpu.SemaphoreType.DMA((32,)),
+        scratch_shapes=scratch + [
+            pltpu.SemaphoreType.DMA((128,)), pltpu.SemaphoreType.DMA((128,)), pltpu.SemaphoreType.DMA((32,)),
         ],
-        compiler_params=pltpu.CompilerParams(collective_id=0, has_side_effects=True, vmem_limit_bytes=60 << 20),
-        name="first",
-    )(hidden, cot, wq, wo, wu, wd, rows, params, bq, freq)
+        compiler_params=pltpu.CompilerParams(collective_id=0, has_side_effects=True, vmem_limit_bytes=62 << 20),
+        name="block",
+    )(hidden, cot, wq, wo, wu, wd, rows, params, bq, bu, freq)
 
 
 def normalize(values):
@@ -905,125 +1107,33 @@
         bq = by_quarter(qkv_bias[None, :]).astype(F32)
         up_half = half_of(up_bias, 0)
         up_row = jnp.concatenate([piece_of(up_half, q, 0) for q in range(quarters)])[None, :].astype(F32)
-        x_all, g_all, a_all, qkv_all, out_all, up_all, down_all, mixes, ctxs, rows_far, params = first(
-            hidden, cotangent, wq, out_weight, up_weight, down_weight, rows_own, params, bq, freq, rows
+        grad_q, grad_o, grad_u, grad_d, keep, near_parts, far_parts, small = whole_block(
+            hidden, cotangent, wq, out_weight, up_weight, down_weight, rows_own, params, bq, up_row, freq, rows
         )
-        gain_one, shift_one, gain_two, shift_two = [params[i][None, :] for i in range(4)]
-        cots = [g_all[0], g_all[1]]
-        norms = []
-        for index in range(2):
-            unit, inv = normalize(x_all[index].astype(F32))
-            norms.append((unit, inv, a_all[index], (unit * gain_two + shift_two).astype(BF16)))
-        contexts = [ctxs[0], ctxs[1]]
-        grads_mixed = [mixes[0], mixes[1]]
-
-        feeds = [feed(norm[3], cot, up_all, up_row, down_all) for norm, cot in zip(norms, cots)]
-
-        def reduce_grad(left, right, width_axis, unit_axis, placed, shape=None):
-            total = dot(left[0], right[0], TN) + dot(left[1], right[1], TN)
-            if shape is not None:
-                total = total.reshape(shape)
-            mine = piece_of(total, 0, unit_axis, placed)
-            for q in range(1, quarters):
-                part = piece_of(total, q, unit_axis, placed).astype(BF16)
-                mine = mine + quarter_shift(part, -q).astype(F32)
-            cut = lambda t: lax.dynamic_slice_in_dim(mine, lax.rem(row + t, rows) * shard, shard, width_axis)
-            result = cut(0)
-            for t in range(1, rows):
-                result = result + row_shift(cut(t).astype(BF16), t).astype(F32)
-            result = result.astype(BF16)
-            pieces = [result] + [quarter_shift(result, q) for q in range(1, quarters)]
-            result = in_place(pieces, unit_axis)
-            far = pair_swap(result)
-            flip = side == 0
-            return jnp.concatenate(
-                [jnp.where(flip, result, far), jnp.where(flip, far, result)], axis=unit_axis
-            ).astype(F32)
-
-        acts_one = [n[2] for n in norms]
-        acts_two = [n[3] for n in norms]
-        out_grad = reduce_grad(contexts, cots, 1, 0, whole_heads)
-        qkv_grad = reduce_grad(acts_one, grads_mixed, 0, 1, True)
-        down_grad = reduce_grad([f[0] for f in feeds], cots, 1, 0, True)
-        up_grad = reduce_grad(acts_two, [f[1] for f in feeds], 0, 1, True)
-        qkv_grad = qkv_grad.reshape(shard, 2 * quarters, 3, heads // quarters, HEAD_DIM)
-        qkv_grad = jnp.swapaxes(qkv_grad, 2, 3).reshape(shard, 6 * wide)
-
-        outs = []
-        slopes = []
-        norm_sums = jnp.zeros((4, width), F32)
-        for index in range(2):
-            unit, inv, _, _ = norms[index]
-            act, grad_up, _ = feeds[index]
-            outs.append((dot(contexts[index], out_all) + dot(act, down_all)).astype(BF16))
-            grad_one = dot(grads_mixed[index], qkv_all, NT)
-            grad_two = dot(grad_up, up_all, NT)
-            norm_sums += jnp.stack(
-                [
-                    jnp.sum(grad_one * unit, axis=0),
-                    jnp.sum(grad_one, axis=0),
-                    jnp.sum(grad_two * unit, axis=0),
-                    jnp.sum(grad_two, axis=0),
-                ]
-            )
-            scaled = grad_one * gain_one + grad_two * gain_two
-            mean_scaled = jnp.mean(scaled, axis=1, keepdims=True)
-            mean_unit = jnp.mean(scaled * unit, axis=1, keepdims=True)
-            slopes.append((inv * (scaled - mean_scaled - unit * mean_unit)).astype(BF16))
-
-        def fold(pair):
-            sums = []
-            for value in pair:
-                kept = lax.dynamic_slice_in_dim(value, col * half_width, half_width, 1).astype(F32)
-                given = lax.dynamic_slice_in_dim(value, (1 - col) * half_width, half_width, 1)
-                sums.append(kept + core_swap(given).astype(F32))
-            return sums[0] + pair_swap(sums[1].astype(BF16)).astype(F32)
-
-        cot_local = cotangent.astype(F32)
-        output = hidden.astype(F32) + fold(outs) + (out_bias.astype(F32) + down_bias.astype(F32))
-        input_grad = cot_local + fold(slopes)
-
-        qkv_sum = (
-            jnp.sum(grads_mixed[0].astype(F32), axis=0) + jnp.sum(grads_mixed[1].astype(F32), axis=0)
-        )
-        qkv_sum = in_place([piece_of(qkv_sum, q, 0, True) for q in range(quarters)], 0)
-        up_sum = (feeds[0][2] + feeds[1][2])[0]
-        up_sum = in_place([piece_of(up_sum, q, 0, True) for q in range(quarters)], 0)
-
-        def widen(value):
-            zeros = jnp.zeros_like(value)
-            flip = side == 0
-            return jnp.concatenate([jnp.where(flip, value, zeros), jnp.where(flip, zeros, value)], axis=-1)
-
-        kept = lax.dynamic_slice_in_dim(norm_sums, col * half_width, half_width, 1)
-        given = lax.dynamic_slice_in_dim(norm_sums, (1 - col) * half_width, half_width, 1)
-        norm_sums = kept + core_swap(given)
-        small = jnp.concatenate(
-            [widen(qkv_sum).reshape(-1), widen(up_sum), jnp.sum(cot_local, axis=0), norm_sums.reshape(-1)]
-        )
-        small = lax.psum(small, ("dp", "row"))
-        sizes = [6 * wide, 2 * units, half_width, half_width, half_width, half_width, half_width]
-        parts = []
-        start = 0
-        for size in sizes:
-            parts.append(lax.slice_in_dim(small, start, start + size))
-            start += size
-        qkv_sum, up_sum, cot_sum, gain_one_sum, shift_one_sum, gain_two_sum, shift_two_sum = parts
-        qkv_sum = jnp.swapaxes(qkv_sum.reshape(2 * quarters, 3, heads // quarters, HEAD_DIM), 1, 2).reshape(-1)
+        heads_of = lambda value, n: jnp.swapaxes(
+            value.reshape(n, 2 * quarters, 3, heads // quarters, HEAD_DIM), 2, 3
+        ).reshape(n, 6 * wide)
+        sums = lambda i: keep[i].astype(F32) + near_parts[i].astype(F32) + far_parts[i].astype(F32)
+        output = hidden.astype(F32) + sums(0) + (out_bias.astype(F32) + down_bias.astype(F32))
+        input_grad = cotangent.astype(F32) + sums(1)
+        qkv_sum = heads_of(jnp.concatenate([small[0, 0, : 3 * wide], small[1, 0, : 3 * wide]])[None, :], 1)[0]
+        up_sum = jnp.concatenate([small[0, 1], small[1, 1]])
+        tail = lax.dynamic_slice_in_dim(small[3, 2:6], col * half_width, half_width, 1)
+        cot_sum = lax.dynamic_slice_in_dim(small[2, 6], col * half_width, half_width, 0)
         return (
             output,
             input_grad,
-            gain_one_sum,
-            shift_one_sum,
-            qkv_grad,
+            tail[0],
+            tail[1],
+            heads_of(grad_q, shard).astype(F32),
             qkv_sum,
-            out_grad,
+            grad_o.astype(F32),
             cot_sum,
-            gain_two_sum,
-            shift_two_sum,
-            up_grad,
+            tail[2],
+            tail[3],
+            grad_u.astype(F32),
             up_sum,
-            down_grad,
+            grad_d.astype(F32),
             cot_sum,
         )
 

time: 481 us -> 256 us (0.53)
  waiting for transfers between devices: 110 us -> 0 us
  Pallas kernels: 117 us -> 225 us
  blocking collectives: 79.6 us -> 0 us
  matrix products: 57.1 us -> 0 us
  starting transfers between devices: 32 us -> 0 us
  other arithmetic: 45.2 us -> 16 us
  local copies, waits for them, and re-layouts: 32.5 us -> 9.49 us
    ppermute x31 -> x0, waiting for transfers between devices: 110 us -> none  [the longest x6 48 us: pair_swap(): return lax.ppermute(value, 'dp', [(d, d ^ 1) for d in range(groups)])]
    pallas_call x3 -> x1, Pallas kernels: 117 us -> 225 us  [whole_block(): pl.pallas_call(functools.partial(block_kernel, rows_n=rows_n), out_shape=...]
    psum x1 -> x0, blocking collectives: 79.6 us -> none  [local(): small = lax.psum(small, ('dp', 'row'))]
    dot_general x16 -> x0, matrix products: 57.1 us -> none  [dot(): return lax.dot_general(a, b, dims, preferred_element_type=F32)]
    ppermute x31 -> x0, starting transfers between devices: 32 us -> none  [the longest x12 16.1 us: row_shift(): lax.ppermute(value, 'row', [(r, (r + shift) % rows) for r in range(rows)])]
    convert_element_type x11 -> x3, other arithmetic: 19 us -> 5.1 us  [the longest x1 2.79 us: local(): grad_u.astype(F32)]
    unnamed x100 -> x33, local copies, waits for them, and re-layouts: 15.8 us -> 4 us
    reduce_sum x4 -> x0, other arithmetic: 9.01 us -> none  [the longest x1 3.4 us: local(): jnp.sum(cot_local, axis=0)]
  transfers between devices with their start and end apart: 31 -> 0, of which waited for: 15 -> 0; matrix products, arithmetic and copies ran while one was open for 19% -> 0% of each run, Pallas kernels for 0% -> 0%
where the time goes in v3:
time: 256 us; the launch traced here: 252 us
  Pallas kernels  225 us (88%)
  other arithmetic  16 us (6%)
  local copies, waits for them, and re-layouts  9.49 us (4%)
    pallas_call x1, Pallas kernels, whole_block(): pl.pallas_call(functools.partial(block_kernel, rows_n=rows_n), out_shape=...  225 us
    add x1, other arithmetic, local(): input_grad = cotangent.astype(F32) + sums(1)  6.34 us

profile of v3, /device:TPU:0, one launch (start us, length us, event | category | flops | bytes accessed | tf_op | source)
XLA Modules:
  0.0 251.6 jit_solution(13351029618244285179)
XLA Ops:
  0.6 1.4 copy.54
  2.3 0.2 copy.63
  2.4 0.2 copy.64
  2.7 0.8 pad_maximum_fusion.wq_in
  3.4 0.6 convert_reduce_fusion
  4.0 0.1 pad.11.clone
  4.1 0.1 pad.10.clone
  4.2 0.7 maximum_maximum_fusion.rows_in
  5.0 0.6 convert_element_type.103.params_in
  5.6 0.1 reshape_broadcast_in_dim.6
  5.7 0.1 reshape.259
  5.8 0.6 maximum_convert_fusion.1.bq_in
  6.4 0.1 fusion.9
  6.5 0.6 maximum_convert_fusion.bu_in
  7.1 0.6 stack.49.freq_in
  7.7 224.9 %block.1 = (bf16[256,1536]{1,0:T(8,128)(2,1)}, bf16[512,256]{1,0:T(8,128)(2,1)}, bf16[256,2048]{1,0:T(8,128)(2,1)}, bf16[2048,256]{1,0:T(8,128)(2,1)}, bf16[2,10...) custom-call(bf16[1024,512]{1,0:T(8,128)(2,1)} %hidden.1, ...), custom_call_target="tpu_custom_call" | custom-call | tf_op jit(solution)/shard_map/block/pallas_call | solution.py:697
  232.8 6.3 %bitcast_add_fusion = (f32[1024,512]{1,0:T(8,128)}, f32[1024,512]{1,0:T(8,128)}) fusion(bf16[1024,512]{1,0:T(8,128)(2,1)S(1)} %copy-done, bf16[2,1024,512]{2,1,0:T(8,128)(2,1)} %get-tuple-element.24, bf16[2,1024,512]{2,1,0:T(8,128)(2,1)} %get-tuple-element.23, bf16[2,1024,512]{2,1,0:T(8,128)(2,1)} %get-tuple-element.22, f32[512]{0:T(512)S(1)} %convert_add_fusion, ...), kind=kLoop, calls=%fused_computation.1 | loop fusion | flops 7864320 | bytes 12584960 | tf_op jit(solution)/shard_map/add | solution.py:1118
  239.1 0.8 slice.78
  239.9 0.7 constant_dynamic-slice_fusion.4
  240.5 0.3 copy.59
  240.8 0.1 copy.60
  241.0 1.6 copy.62
  242.6 0.9 slice_reduce_fusion.1
  243.5 0.1 reshape_broadcast_in_dim.7
  243.5 0.7 squeeze_reshape.3
  244.2 0.8 convert_element_type.120
  245.1 0.8 fusion.8
  245.9 0.0 copy-start.5
  245.9 2.8 %convert_element_type.121 = f32[256,2048]{1,0:T(8,128)} convert(bf16[256,2048]{1,0:T(8,128)(2,1)} %get-tuple-element.28) | non-fusion elementwise | flops 524288 | bytes 3145728 | tf_op jit(solution)/shard_map/convert_element_type | solution.py:1134
  248.7 0.6 pad_maximum_fusion.2
  249.3 1.5 convert_element_type.122
  250.8 0.6 copy.68
  (50 shorter events, 0.4 us)
Async XLA Ops:
  2.1 1.3 copy-start.4
  2.1 2.8 %copy-start.7 = (bf16[512]{0:T(512)(128)(2,1)S(1)}, bf16[512]{0:T(512)(128)(2,1)}, u32[]{:S(2)}) copy-start(bf16[512]{0:T(512)(128)(2,1)} %param.17) | copy-start | bytes 3076
  2.1 2.8 %copy-start.8 = (bf16[512]{0:T(512)(128)(2,1)S(1)}, bf16[512]{0:T(512)(128)(2,1)}, u32[]{:S(2)}) copy-start(bf16[512]{0:T(512)(128)(2,1)} %param.18) | copy-start | bytes 3076
  2.1 2.8 %copy-start.9 = (bf16[512]{0:T(512)(128)(2,1)S(1)}, bf16[512]{0:T(512)(128)(2,1)}, u32[]{:S(2)}) copy-start(bf16[512]{0:T(512)(128)(2,1)} %param.23) | copy-start | bytes 3076
  2.2 2.8 %copy-start.10 = (bf16[512]{0:T(512)(128)(2,1)S(1)}, bf16[512]{0:T(512)(128)(2,1)}, u32[]{:S(2)}) copy-start(bf16[512]{0:T(512)(128)(2,1)} %param.24) | copy-start | bytes 3076
  2.2 3.5 %copy-start.6 = (bf16[1536]{0:T(1024)(128)(2,1)S(1)}, bf16[1536]{0:T(1024)(128)(2,1)}, u32[]{:S(2)}) copy-start(bf16[1536]{0:T(1024)(128)(2,1)} %param.20) | copy-start | bytes 9220
  2.2 4.2 %copy-start.11 = (bf16[2048]{0:T(1024)(128)(2,1)S(1)}, bf16[2048]{0:T(1024)(128)(2,1)}, u32[]{:S(2)}) copy-start(bf16[2048]{0:T(1024)(128)(2,1)} %param.26) | copy-start | bytes 12292
  7.7 225.0 %copy-start.12 = (bf16[512]{0:T(512)(128)(2,1)S(1)}, bf16[512]{0:T(512)(128)(2,1)}, u32[]{:S(2)}) copy-start(bf16[512]{0:T(512)(128)(2,1)} %param.28) | copy-start | bytes 3076
  7.7 225.0 %copy-start.13 = (bf16[512]{0:T(512)(128)(2,1)S(1)}, bf16[512]{0:T(512)(128)(2,1)}, u32[]{:S(2)}) copy-start(bf16[512]{0:T(512)(128)(2,1)} %param.22) | copy-start | bytes 3076
  7.7 225.0 %copy-start = (bf16[1024,512]{1,0:T(8,128)(2,1)S(1)}, bf16[1024,512]{1,0:T(8,128)(2,1)}, u32[]{:S(2)}) copy-start(bf16[1024,512]{1,0:T(8,128)(2,1)} %cot.1) | copy-start | bytes 3145732
  232.7 7.8 %copy-start.2 = (bf16[256,1536]{1,0:T(8,128)(2,1)S(1)}, bf16[256,1536]{1,0:T(8,128)(2,1)}, u32[]{:S(2)}) copy-start(bf16[256,1536]{1,0:T(8,128)(2,1)} %get-tuple-element.26) | copy-start | bytes 2359300
  241.0 3.3 %copy-start.3 = (bf16[512,256]{1,0:T(8,128)(2,1)S(1)}, bf16[512,256]{1,0:T(8,128)(2,1)}, u32[]{:S(2)}) copy-start(bf16[512,256]{1,0:T(8,128)(2,1)} %get-tuple-element.27) | copy-start | bytes 786436
  242.6 6.7 %copy-start.1 = (bf16[2048,256]{1,0:T(8,128)(2,1)S(1)}, bf16[2048,256]{1,0:T(8,128)(2,1)}, u32[]{:S(2)}) copy-start(bf16[2048,256]{1,0:T(8,128)(2,1)} %get-tuple-element.29) | copy-start | bytes 3145732
  245.9 4.9 %copy-start.5 = (f32[1,1,512]{2,1,0:T(1,128)}, f32[1,1,512]{2,1,0:T(1,128)S(1)}, u32[]{:S(2)}) copy-start(f32[1,1,512]{2,1,0:T(1,128)S(1)} %constant_dynamic-slice_fusion.3) | copy-start | bytes 6148
